TPU v7x, 512 devices: a whole 4x4x16 slice. The times are simulated.
512 devices in a mesh: theta: 16 (over x, y), rad: 32 (over z, core).
Axes of the slice: x: 4, y: 4, z: 16, core: 2. Of those that a mesh axis runs over, the one named last changes fastest.
Arguments:
- pressure_source: float32 [8, 1024, 4096], P(None, 'rad', 'theta'), may hold values from -15 to 15
- conductance: float32 [8, 1024, 4096], P(None, 'rad', 'theta'), may hold values from 0.3 to 3
- slide: int32 [1], replicated, may hold values from 2048 to 2303
- slide_fraction: float32 [1], replicated, may hold values from 0.1 to 0.9
- interface_gain: float32 [1], replicated, may hold values from 0.5 to 4
Outputs:
- pressure: float32 [8, 1024, 4096], P(None, 'rad', 'theta')
- residual: float32 [8, 1024, 4096], P(None, 'rad', 'theta')
All inputs are finite; a program needn't handle non-finite values.
Results may differ from a plain program's by a relative error of at most 0.0003.
Values sent between devices are 32-bit elements; how exact they have to be, the bound alone decides.
A program may use at most 64 MiB of HBM per device.

v0:
```python
import jax
import jax.numpy as jnp
from jax import lax
from jax.sharding import PartitionSpec as P

LEVELS = 5
COARSE_SWEEPS = 4


relaxation = 0.8


def with_halo(value, sides, width):
    for axis, dim in sides:
        peers, length = (lax.axis_size(axis), value.shape[dim])
        up = [(i, (i + 1) % peers) for i in range(peers)]
        down = [(j, i) for i, j in up]
        last = lax.slice_in_dim(value, length - width, length, axis=dim)
        initial = lax.slice_in_dim(value, 0, width, axis=dim)
        before = lax.ppermute(last, axis, up)
        after = lax.ppermute(initial, axis, down)
        value = jnp.concatenate([before, value, after], axis=dim)
    return value


def coarsen(values):
    shape = values.shape
    return values.reshape(shape[0], shape[1] // 2, 2, shape[2] // 2, 2).sum(axis=(2, 4))


def prolong(values):
    return jnp.repeat(jnp.repeat(values, 2, axis=1), 2, axis=2)


def face_coefs(conduct_pad, row_index, rows_level, gain_value, upper_mask, lower_mask):
    conduct = conduct_pad[:, 1:-1, 1:-1]
    position = row_index.astype(jnp.float32)
    radius_cell = (1.0 + (position + 0.5) / rows_level)[None, :, None]
    radius_upper = (1.0 + (position + 1.0) / rows_level)[None, :, None]
    radius_lower = (1.0 + position / rows_level)[None, :, None]
    upper_plain = 0.5 * (conduct + conduct_pad[:, 2:, 1:-1]) * radius_upper
    lower_plain = 0.5 * (conduct + conduct_pad[:, :-2, 1:-1]) * radius_lower
    upper_coef = jnp.where(upper_mask[None, :, None], gain_value * upper_plain, upper_plain)
    lower_coef = jnp.where(lower_mask[None, :, None], gain_value * lower_plain, lower_plain)
    east_coef = 0.5 * (conduct + conduct_pad[:, 1:-1, 2:]) / radius_cell
    west_coef = 0.5 * (conduct + conduct_pad[:, 1:-1, :-2]) / radius_cell
    axial_coef = 0.5 * (conduct[1:] + conduct[:-1]) * radius_cell
    diagonal = upper_coef + lower_coef + east_coef + west_coef
    diagonal = (
        diagonal
        + jnp.pad(axial_coef, ((0, 1), (0, 0), (0, 0)))
        + jnp.pad(axial_coef, ((1, 0), (0, 0), (0, 0)))
    )
    return (upper_coef, lower_coef, east_coef, west_coef, axial_coef, diagonal)


def remap(stator_row, rotor_row, slide_cells, fraction):
    rotor_side = (1.0 - fraction) * jnp.roll(
        stator_row, -slide_cells, axis=1
    ) + fraction * jnp.roll(stator_row, -slide_cells - 1, axis=1)
    stator_side = (1.0 - fraction) * jnp.roll(rotor_row, slide_cells, axis=1) + fraction * jnp.roll(
        rotor_row, slide_cells + 1, axis=1
    )
    return (rotor_side, stator_side)


def apply_operator(field_pad, coeffs, rotor_side, stator_side, upper_mask, lower_mask):
    upper_coef, lower_coef, east_coef, west_coef, axial_coef, diagonal = coeffs
    field = field_pad[:, 1:-1, 1:-1]
    upper_values = jnp.where(
        upper_mask[None, :, None], rotor_side[:, None, :], field_pad[:, 2:, 1:-1]
    )
    lower_values = jnp.where(
        lower_mask[None, :, None], stator_side[:, None, :], field_pad[:, :-2, 1:-1]
    )
    axial_flux = axial_coef * (field[1:] - field[:-1])
    axial_term = jnp.pad(axial_flux, ((1, 0), (0, 0), (0, 0))) - jnp.pad(
        axial_flux, ((0, 1), (0, 0), (0, 0))
    )
    result = upper_coef * (field - upper_values) + lower_coef * (field - lower_values)
    result = (
        result
        + east_coef * (field - field_pad[:, 1:-1, 2:])
        + west_coef * (field - field_pad[:, 1:-1, :-2])
    )
    return result + axial_term


def clear_ends(padded, radial_rank, radial_devices):
    row_index = jnp.arange(padded.shape[1], dtype=jnp.int32)
    outside = (row_index == 0) & (radial_rank == 0) | (row_index == padded.shape[1] - 1) & (
        radial_rank == radial_devices - 1
    )
    return jnp.where(outside[None, :, None], jnp.zeros_like(padded), padded)


def on_device(pressure_source, conductance, slide, slide_fraction, interface_gain):
    radial_devices = lax.axis_size("rad")
    radial_rank = lax.axis_index("rad")
    azimuth_rank = lax.axis_index("theta")
    slide_cells = slide[0]
    fraction = slide_fraction[0]
    gain_value = interface_gain[0]
    conducts = [conductance]
    for level_index in range(1, LEVELS):
        conducts.append(0.25 * coarsen(conducts[-1]))

    def local_operator(level_index):
        conduct = conducts[level_index]
        rows_local = conduct.shape[1]
        rows_level = rows_local * radial_devices
        row_index = radial_rank * rows_local + jnp.arange(rows_local, dtype=jnp.int32)
        upper_mask = row_index == rows_level // 2 - 1
        lower_mask = row_index == rows_level // 2
        conduct_pad = with_halo(conduct, (("theta", 2), ("rad", 1)), 1)
        conduct_pad = clear_ends(conduct_pad, radial_rank, radial_devices)
        coeffs = face_coefs(conduct_pad, row_index, rows_level, gain_value, upper_mask, lower_mask)
        return (coeffs, upper_mask, lower_mask, slide_cells // 2**level_index)

    def local_apply(field, operator):
        coeffs, upper_mask, lower_mask, cells = operator
        field_pad = with_halo(field, (("theta", 2), ("rad", 1)), 1)
        field_pad = clear_ends(field_pad, radial_rank, radial_devices)
        rim_rows = jnp.stack([field_pad[:, -1, 1:-1], field_pad[:, 0, 1:-1]])
        gathered = lax.all_gather(rim_rows, "theta", axis=2, tiled=True)
        rotor_side, stator_side = remap(gathered[0], gathered[1], cells, fraction)
        block_width = field.shape[2]
        rotor_side = lax.dynamic_slice_in_dim(
            rotor_side, azimuth_rank * block_width, block_width, 1
        )
        stator_side = lax.dynamic_slice_in_dim(
            stator_side, azimuth_rank * block_width, block_width, 1
        )
        return apply_operator(field_pad, coeffs, rotor_side, stator_side, upper_mask, lower_mask)

    operators = [local_operator(level_index) for level_index in range(LEVELS - 1)]

    def coarse_solve(source):
        operator = local_operator(LEVELS - 1)
        diagonal = operator[0][5]
        field = relaxation * source / diagonal
        for sweep_index in range(COARSE_SWEEPS - 1):
            field = field + relaxation * (source - local_apply(field, operator)) / diagonal
        return field

    def vcycle(level_index, source):
        if level_index == LEVELS - 1:
            return coarse_solve(source)
        operator = operators[level_index]
        diagonal = operator[0][5]
        field = relaxation * source / diagonal
        remainder = source - local_apply(field, operator)
        field = field + prolong(vcycle(level_index + 1, coarsen(remainder)))
        return field + relaxation * (source - local_apply(field, operator)) / diagonal

    pressure = vcycle(0, pressure_source)
    residual = pressure_source - local_apply(pressure, operators[0])
    return (pressure, residual)


def solution(mesh):
    in_specs = (P(None, "rad", "theta"), P(None, "rad", "theta"), P(), P(), P())
    out_specs = (P(None, "rad", "theta"), P(None, "rad", "theta"))
    return jax.shard_map(
        on_device, mesh=mesh, in_specs=in_specs, out_specs=out_specs, check_vma=False
    )
```

profile of v0, /device:TPU:4, one launch (start us, length us, event | category | flops | bytes accessed | tf_op | source)
XLA Modules:
  0.0 626.9 jit_solution(7496580535165126100)
XLA Ops:
  1.8 4.9 collective-permute-start.1
  8.7 3.5 copy.554
  12.2 5.8 reduce_sum.73
  18.4 6.0 collective-permute-start.9
  41.2 3.9 collective-permute-start.32
  45.2 3.6 collective-permute-done.32
  50.9 6.0 collective-permute-start.17
  61.0 3.9 collective-permute-done.16
  64.9 5.2 collective-permute-start.35
  70.9 4.4 collective-permute-start.27
  83.1 2.9 collective-permute-done.2
  90.0 3.1 collective-permute-start.4
  94.1 4.8 collective-permute-done.4
  104.1 27.9 %all_gather.36 = f32[2,8,4096]{2,1,0:T(8,128)S(1)} all-gather(f32[2,8,256]{2,1,0:T(8,128)S(1)} %pad_maximum_fusion.5), channel_id=1, replica_groups=mesh['theta'=16,'rad'=32] {'theta'}, dimensions={2}, use_global_device_ids=true | all-gather | bytes 278528 | tf_op jit(solution)/shard_map/all_gather | solution.py:125
  135.3 5.8 reduce_sum.72
  142.5 4.0 collective-permute-start.13
  149.3 5.4 collective-permute-done.12
  160.9 23.3 %all_gather.37 = f32[2,8,2048]{2,1,0:T(8,128)S(1)} all-gather(f32[2,8,128]{2,1,0:T(8,128)S(1)} %pad_maximum_fusion.33), channel_id=1, replica_groups=mesh['theta'=16,'rad'=32] {'theta'}, dimensions={2}, use_global_device_ids=true | all-gather | bytes 139264 | tf_op jit(solution)/shard_map/all_gather | solution.py:125
  191.4 4.0 collective-permute-start.21
  198.3 5.0 collective-permute-done.20
  210.0 24.3 %all_gather.38 = f32[2,8,1024]{1,0,2:T(2,128)S(1)} all-gather(f32[2,8,64]{1,0,2:T(2,128)S(1)} %copy.561), channel_id=1, replica_groups=mesh['theta'=16,'rad'=32] {'theta'}, dimensions={2}, use_global_device_ids=true | all-gather | bytes 69632 | tf_op jit(solution)/shard_map/all_gather | solution.py:125
  240.4 4.4 collective-permute-start.29
  246.9 5.5 collective-permute-done.28
  259.3 23.2 %all_gather.39 = f32[2,8,512]{1,0,2:T(2,128)S(1)} all-gather(f32[2,8,32]{1,0,2:T(2,128)S(1)} %copy.581), channel_id=1, replica_groups=mesh['theta'=16,'rad'=32] {'theta'}, dimensions={2}, use_global_device_ids=true | all-gather | bytes 34816 | tf_op jit(solution)/shard_map/all_gather | solution.py:125
  285.4 4.5 collective-permute-start.37
  291.9 5.5 collective-permute-done.36
  303.8 22.0 %all_gather.40 = f32[2,8,256]{1,0,2:T(2,128)S(1)} all-gather(f32[2,8,16]{1,0,2:T(2,128)S(1)} %copy.602), channel_id=1, replica_groups=mesh['theta'=16,'rad'=32] {'theta'}, dimensions={2}, use_global_device_ids=true | all-gather | bytes 17408 | tf_op jit(solution)/shard_map/all_gather | solution.py:125
  326.6 4.6 collective-permute-start.41
  333.2 5.5 collective-permute-done.40
  343.8 22.6 %all_gather.41 = f32[2,8,256]{1,0,2:T(2,128)S(1)} all-gather(f32[2,8,16]{1,0,2:T(2,128)S(1)} %copy.619), channel_id=1, replica_groups=mesh['theta'=16,'rad'=32] {'theta'}, dimensions={2}, use_global_device_ids=true | all-gather | bytes 17408 | tf_op jit(solution)/shard_map/all_gather | solution.py:125
  367.3 4.6 collective-permute-start.45
  373.9 5.5 collective-permute-done.44
  384.4 22.0 %all_gather.42 = f32[2,8,256]{1,0,2:T(2,128)S(1)} all-gather(f32[2,8,16]{1,0,2:T(2,128)S(1)} %copy.636), channel_id=1, replica_groups=mesh['theta'=16,'rad'=32] {'theta'}, dimensions={2}, use_global_device_ids=true | all-gather | bytes 17408 | tf_op jit(solution)/shard_map/all_gather | solution.py:125
  407.3 4.6 collective-permute-start.49
  413.9 5.5 collective-permute-done.48
  424.4 23.0 %all_gather.43 = f32[2,8,512]{1,0,2:T(2,128)S(1)} all-gather(f32[2,8,32]{1,0,2:T(2,128)S(1)} %copy.651), channel_id=1, replica_groups=mesh['theta'=16,'rad'=32] {'theta'}, dimensions={2}, use_global_device_ids=true | all-gather | bytes 34816 | tf_op jit(solution)/shard_map/all_gather | solution.py:125
  449.8 4.5 collective-permute-start.53
  456.2 6.0 collective-permute-done.52
  467.7 23.1 %all_gather.44 = f32[2,8,1024]{1,0,2:T(2,128)S(1)} all-gather(f32[2,8,64]{1,0,2:T(2,128)S(1)} %copy.665), channel_id=1, replica_groups=mesh['theta'=16,'rad'=32] {'theta'}, dimensions={2}, use_global_device_ids=true | all-gather | bytes 69632 | tf_op jit(solution)/shard_map/all_gather | solution.py:125
  493.7 4.6 collective-permute-start.57
  500.2 6.3 %collective-permute-done.56 = f32[8,16,1]{2,1,0:T(8,128)S(1)} collective-permute-done((f32[8,16,1]{2,1,0:T(8,128)S(1)}, f32[8,16,1]{2,1,0:T(8,128)S(1)}, u32[]{:S(2)}, u32[]{:S(2)}) %collective-permute-start.56) | collective-permute-done | bytes 544 | tf_op jit(solution)/shard_map/ppermute | solution.py:20
  512.7 22.0 %all_gather.45 = f32[2,8,2048]{2,1,0:T(8,128)S(1)} all-gather(f32[2,8,128]{2,1,0:T(8,128)S(1)} %pad_maximum_fusion.43), channel_id=1, replica_groups=mesh['theta'=16,'rad'=32] {'theta'}, dimensions={2}, use_global_device_ids=true | all-gather | bytes 139264 | tf_op jit(solution)/shard_map/all_gather | solution.py:125
  540.5 4.0 collective-permute-start.61
  547.4 6.1 collective-permute-done.60
  558.6 23.4 %all_gather.46 = f32[2,8,4096]{2,1,0:T(8,128)S(1)} all-gather(f32[2,8,256]{2,1,0:T(8,128)S(1)} %pad_maximum_fusion.10), channel_id=1, replica_groups=mesh['theta'=16,'rad'=32] {'theta'}, dimensions={2}, use_global_device_ids=true | all-gather | bytes 278528 | tf_op jit(solution)/shard_map/all_gather | solution.py:125
  582.9 5.6 collective-permute-start.65
  590.9 6.5 %collective-permute-done.64 = f32[8,32,1]{2,0,1:T(8,128)S(1)} collective-permute-done((f32[8,32,1]{2,0,1:T(8,128)S(1)}, f32[8,32,1]{2,0,1:T(8,128)S(1)}, u32[]{:S(2)}, u32[]{:S(2)}) %collective-permute-start.64) | collective-permute-done | bytes 1056 | tf_op jit(solution)/shard_map/ppermute | solution.py:20
  602.5 22.7 %all_gather.47 = f32[2,8,4096]{2,1,0:T(8,128)S(1)} all-gather(f32[2,8,256]{2,1,0:T(8,128)S(1)} %pad_maximum_fusion.11), channel_id=1, replica_groups=mesh['theta'=16,'rad'=32] {'theta'}, dimensions={2}, use_global_device_ids=true | all-gather | bytes 278528 | tf_op jit(solution)/shard_map/all_gather | solution.py:125
  (463 shorter events, 166.5 us)
Async XLA Ops:
  1.8 76.8 %collective-permute-start.1 = (f32[8,32,1]{2,0,1:T(8,128)S(1)}, f32[8,32,1]{2,0,1:T(8,128)S(1)}, u32[]{:S(2)}, u32[]{:S(2)}) collective-permute-start(f32[8,32,1]{2,0,1:T(8,128)S(1)} %get-tuple-element.89), channel_id=1, source_target_pairs={{32,0},{64,32},{96,64},{128,96},{160,128},{192,160},{224,192},{256... | collective-permute-start | bytes 3080 | tf_op jit(solution)/shard_map/ppermute | solution.py:21
  6.7 71.9 %collective-permute-start = (f32[8,32,1]{2,0,1:T(8,128)S(1)}, f32[8,32,1]{2,0,1:T(8,128)S(1)}, u32[]{:S(2)}, u32[]{:S(2)}) collective-permute-start(f32[8,32,1]{2,0,1:T(8,128)S(1)} %get-tuple-element.88), channel_id=1, source_target_pairs={{0,32},{32,64},{64,96},{96,128},{128,160},{160,192},{192,224},{224... | collective-permute-start | bytes 3080 | tf_op jit(solution)/shard_map/ppermute | solution.py:20
  18.4 52.5 %collective-permute-start.9 = (f32[8,16,1]{2,1,0:T(8,128)S(1)}, f32[8,16,1]{2,1,0:T(8,128)S(1)}, u32[]{:S(2)}, u32[]{:S(2)}) collective-permute-start(f32[8,16,1]{2,1,0:T(8,128)S(1)} %get-tuple-element.129), channel_id=1, source_target_pairs={{32,0},{64,32},{96,64},{128,96},{160,128},{192,160},{224,192},{256... | collective-permute-start | bytes 1544 | tf_op jit(solution)/shard_map/ppermute | solution.py:21
  26.1 24.8 %collective-permute-start.25 = (f32[8,4,1]{0,2,1:T(1,128)S(1)}, f32[8,4,1]{0,2,1:T(1,128)S(1)}, u32[]{:S(2)}, u32[]{:S(2)}) collective-permute-start(f32[8,4,1]{0,2,1:T(1,128)S(1)} %get-tuple-element.123), channel_id=1, source_target_pairs={{32,0},{64,32},{96,64},{128,96},{160,128},{192,160},{224,192},{256... | collective-permute-start | bytes 392 | tf_op jit(solution)/shard_map/ppermute | solution.py:21
  28.2 13.1 %collective-permute-start.33 = (f32[8,2,1]{0,2,1:T(1,128)S(1)}, f32[8,2,1]{0,2,1:T(1,128)S(1)}, u32[]{:S(2)}, u32[]{:S(2)}) collective-permute-start(f32[8,2,1]{0,2,1:T(1,128)S(1)} %get-tuple-element.155), channel_id=1, source_target_pairs={{32,0},{64,32},{96,64},{128,96},{160,128},{192,160},{224,192},{256... | collective-permute-start | bytes 200 | tf_op jit(solution)/shard_map/ppermute | solution.py:21
  41.2 7.6 %collective-permute-start.32 = (f32[8,2,1]{0,2,1:T(1,128)S(1)}, f32[8,2,1]{0,2,1:T(1,128)S(1)}, u32[]{:S(2)}, u32[]{:S(2)}) collective-permute-start(f32[8,2,1]{0,2,1:T(1,128)S(1)} %get-tuple-element.154), channel_id=1, source_target_pairs={{0,32},{32,64},{64,96},{96,128},{128,160},{160,192},{192,224},{224... | collective-permute-start | bytes 200 | tf_op jit(solution)/shard_map/ppermute | solution.py:20
  48.8 8.2 %collective-permute-start.24 = (f32[8,4,1]{0,2,1:T(1,128)S(1)}, f32[8,4,1]{0,2,1:T(1,128)S(1)}, u32[]{:S(2)}, u32[]{:S(2)}) collective-permute-start(f32[8,4,1]{0,2,1:T(1,128)S(1)} %get-tuple-element.122), channel_id=1, source_target_pairs={{0,32},{32,64},{64,96},{96,128},{128,160},{160,192},{192,224},{224... | collective-permute-start | bytes 392 | tf_op jit(solution)/shard_map/ppermute | solution.py:20
  50.9 8.2 %collective-permute-start.17 = (f32[8,8,1]{2,1,0:T(8,128)S(1)}, f32[8,8,1]{2,1,0:T(8,128)S(1)}, u32[]{:S(2)}, u32[]{:S(2)}) collective-permute-start(f32[8,8,1]{2,1,0:T(8,128)S(1)} %get-tuple-element.147), channel_id=1, source_target_pairs={{32,0},{64,32},{96,64},{128,96},{160,128},{192,160},{224,192},{256... | collective-permute-start | bytes 776 | tf_op jit(solution)/shard_map/ppermute | solution.py:21
  57.0 7.9 %collective-permute-start.16 = (f32[8,8,1]{2,1,0:T(8,128)S(1)}, f32[8,8,1]{2,1,0:T(8,128)S(1)}, u32[]{:S(2)}, u32[]{:S(2)}) collective-permute-start(f32[8,8,1]{2,1,0:T(8,128)S(1)} %get-tuple-element.146), channel_id=1, source_target_pairs={{0,32},{32,64},{64,96},{96,128},{128,160},{160,192},{192,224},{224... | collective-permute-start | bytes 776 | tf_op jit(solution)/shard_map/ppermute | solution.py:20
  59.1 11.8 %collective-permute-start.8 = (f32[8,16,1]{2,1,0:T(8,128)S(1)}, f32[8,16,1]{2,1,0:T(8,128)S(1)}, u32[]{:S(2)}, u32[]{:S(2)}) collective-permute-start(f32[8,16,1]{2,1,0:T(8,128)S(1)} %get-tuple-element.128), channel_id=1, source_target_pairs={{0,32},{32,64},{64,96},{96,128},{128,160},{160,192},{192,224},{224... | collective-permute-start | bytes 1544 | tf_op jit(solution)/shard_map/ppermute | solution.py:20
  64.9 10.5 %collective-permute-start.35 = (f32[8,1,18]{2,0,1:T(8,128)S(1)}, f32[8,1,18]{2,0,1:T(8,128)S(1)}, u32[]{:S(2)}, u32[]{:S(2)}) collective-permute-start(f32[8,1,18]{2,0,1:T(8,128)S(1)} %get-tuple-element.163), channel_id=1, source_target_pairs={{1,0},{2,1},{3,2},{4,3},{5,4},{6,5},{7,6},{8,7},{9,8},{10,9},{11,1... | collective-permute-start | bytes 1736 | tf_op jit(solution)/shard_map/ppermute | solution.py:21
  70.9 5.7 collective-permute-start.34
  70.9 10.8 %collective-permute-start.27 = (f32[8,1,34]{2,0,1:T(8,128)S(1)}, f32[8,1,34]{2,0,1:T(8,128)S(1)}, u32[]{:S(2)}, u32[]{:S(2)}) collective-permute-start(f32[8,1,34]{2,0,1:T(8,128)S(1)} %get-tuple-element.141), channel_id=1, source_target_pairs={{1,0},{2,1},{3,2},{4,3},{5,4},{6,5},{7,6},{8,7},{9,8},{10,9},{11,1... | collective-permute-start | bytes 3272 | tf_op jit(solution)/shard_map/ppermute | solution.py:21
  75.4 6.3 %collective-permute-start.26 = (f32[8,1,34]{2,0,1:T(8,128)S(1)}, f32[8,1,34]{2,0,1:T(8,128)S(1)}, u32[]{:S(2)}, u32[]{:S(2)}) collective-permute-start(f32[8,1,34]{2,0,1:T(8,128)S(1)} %get-tuple-element.140), channel_id=1, source_target_pairs={{0,1},{1,2},{2,3},{3,4},{4,5},{5,6},{6,7},{7,8},{8,9},{9,10},{10,1... | collective-permute-start | bytes 3272 | tf_op jit(solution)/shard_map/ppermute | solution.py:20
  76.5 71.9 %collective-permute-start.19 = (f32[8,1,66]{2,1,0:T(1,128)}, f32[8,1,66]{2,1,0:T(1,128)}, u32[]{:S(2)}, u32[]{:S(2)}) collective-permute-start(f32[8,1,66]{2,1,0:T(1,128)} %get-tuple-element.113), channel_id=1, source_target_pairs={{1,0},{2,1},{3,2},{4,3},{5,4},{6,5},{7,6},{8,7},{9,8},{10,9},{11,1... | collective-permute-start | bytes 6344 | tf_op jit(solution)/shard_map/ppermute | solution.py:21
  78.6 69.8 %collective-permute-start.18 = (f32[8,1,66]{2,1,0:T(1,128)}, f32[8,1,66]{2,1,0:T(1,128)}, u32[]{:S(2)}, u32[]{:S(2)}) collective-permute-start(f32[8,1,66]{2,1,0:T(1,128)} %get-tuple-element.112), channel_id=1, source_target_pairs={{0,1},{1,2},{2,3},{3,4},{4,5},{5,6},{6,7},{7,8},{8,9},{9,10},{10,1... | collective-permute-start | bytes 6344 | tf_op jit(solution)/shard_map/ppermute | solution.py:20
  78.7 11.3 %collective-permute-start.11 = (f32[8,1,130]{2,1,0:T(1,128)S(1)}, f32[8,1,130]{2,1,0:T(1,128)S(1)}, u32[]{:S(2)}, u32[]{:S(2)}) collective-permute-start(f32[8,1,130]{2,1,0:T(1,128)S(1)} %get-tuple-element.99), channel_id=1, source_target_pairs={{1,0},{2,1},{3,2},{4,3},{5,4},{6,5},{7,6},{8,7},{9,8},{10,9},{11,1... | collective-permute-start | bytes 12488 | tf_op jit(solution)/shard_map/ppermute | solution.py:21
  81.7 4.3 collective-permute-start.2
  83.1 10.0 %collective-permute-start.10 = (f32[8,1,130]{2,1,0:T(1,128)S(1)}, f32[8,1,130]{2,1,0:T(1,128)S(1)}, u32[]{:S(2)}, u32[]{:S(2)}) collective-permute-start(f32[8,1,130]{2,1,0:T(1,128)S(1)} %get-tuple-element.98), channel_id=1, source_target_pairs={{0,1},{1,2},{2,3},{3,4},{4,5},{5,6},{6,7},{7,8},{8,9},{9,10},{10,1... | collective-permute-start | bytes 12488 | tf_op jit(solution)/shard_map/ppermute | solution.py:20
  87.2 6.9 %collective-permute-start.5 = (f32[8,32,1]{2,0,1:T(8,128)S(1)}, f32[8,32,1]{2,0,1:T(8,128)S(1)}, u32[]{:S(2)}, u32[]{:S(2)}) collective-permute-start(f32[8,32,1]{2,0,1:T(8,128)S(1)} %get-tuple-element.87), channel_id=1, source_target_pairs={{32,0},{64,32},{96,64},{128,96},{160,128},{192,160},{224,192},{256... | collective-permute-start | bytes 3080 | tf_op jit(solution)/shard_map/ppermute | solution.py:21
  90.0 9.0 %collective-permute-start.4 = (f32[8,32,1]{2,0,1:T(8,128)S(1)}, f32[8,32,1]{2,0,1:T(8,128)S(1)}, u32[]{:S(2)}, u32[]{:S(2)}) collective-permute-start(f32[8,32,1]{2,0,1:T(8,128)S(1)} %get-tuple-element.86), channel_id=1, source_target_pairs={{0,32},{32,64},{64,96},{96,128},{128,160},{160,192},{192,224},{224... | collective-permute-start | bytes 3080 | tf_op jit(solution)/shard_map/ppermute | solution.py:20
  99.0 4.3 collective-permute-start.6
  142.5 6.8 %collective-permute-start.13 = (f32[8,16,1]{2,1,0:T(8,128)S(1)}, f32[8,16,1]{2,1,0:T(8,128)S(1)}, u32[]{:S(2)}, u32[]{:S(2)}) collective-permute-start(f32[8,16,1]{2,1,0:T(8,128)S(1)} %get-tuple-element.127), channel_id=1, source_target_pairs={{32,0},{64,32},{96,64},{128,96},{160,128},{192,160},{224,192},{256... | collective-permute-start | bytes 1544 | tf_op jit(solution)/shard_map/ppermute | solution.py:21
  146.5 8.3 %collective-permute-start.12 = (f32[8,16,1]{2,1,0:T(8,128)S(1)}, f32[8,16,1]{2,1,0:T(8,128)S(1)}, u32[]{:S(2)}, u32[]{:S(2)}) collective-permute-start(f32[8,16,1]{2,1,0:T(8,128)S(1)} %get-tuple-element.126), channel_id=1, source_target_pairs={{0,32},{32,64},{64,96},{96,128},{128,160},{160,192},{192,224},{224... | collective-permute-start | bytes 1544 | tf_op jit(solution)/shard_map/ppermute | solution.py:20
  154.9 4.3 collective-permute-start.14
  191.4 6.9 %collective-permute-start.21 = (f32[8,8,1]{2,1,0:T(8,128)S(1)}, f32[8,8,1]{2,1,0:T(8,128)S(1)}, u32[]{:S(2)}, u32[]{:S(2)}) collective-permute-start(f32[8,8,1]{2,1,0:T(8,128)S(1)} %get-tuple-element.145), channel_id=1, source_target_pairs={{32,0},{64,32},{96,64},{128,96},{160,128},{192,160},{224,192},{256... | collective-permute-start | bytes 776 | tf_op jit(solution)/shard_map/ppermute | solution.py:21
  195.4 7.9 %collective-permute-start.20 = (f32[8,8,1]{2,1,0:T(8,128)S(1)}, f32[8,8,1]{2,1,0:T(8,128)S(1)}, u32[]{:S(2)}, u32[]{:S(2)}) collective-permute-start(f32[8,8,1]{2,1,0:T(8,128)S(1)} %get-tuple-element.144), channel_id=1, source_target_pairs={{0,32},{32,64},{64,96},{96,128},{128,160},{160,192},{192,224},{224... | collective-permute-start | bytes 776 | tf_op jit(solution)/shard_map/ppermute | solution.py:20
  240.4 6.4 %collective-permute-start.29 = (f32[8,4,1]{0,2,1:T(1,128)S(1)}, f32[8,4,1]{0,2,1:T(1,128)S(1)}, u32[]{:S(2)}, u32[]{:S(2)}) collective-permute-start(f32[8,4,1]{0,2,1:T(1,128)S(1)} %get-tuple-element.121), channel_id=1, source_target_pairs={{32,0},{64,32},{96,64},{128,96},{160,128},{192,160},{224,192},{256... | collective-permute-start | bytes 392 | tf_op jit(solution)/shard_map/ppermute | solution.py:21
  244.9 7.6 %collective-permute-start.28 = (f32[8,4,1]{0,2,1:T(1,128)S(1)}, f32[8,4,1]{0,2,1:T(1,128)S(1)}, u32[]{:S(2)}, u32[]{:S(2)}) collective-permute-start(f32[8,4,1]{0,2,1:T(1,128)S(1)} %get-tuple-element.120), channel_id=1, source_target_pairs={{0,32},{32,64},{64,96},{96,128},{128,160},{160,192},{192,224},{224... | collective-permute-start | bytes 392 | tf_op jit(solution)/shard_map/ppermute | solution.py:20
  285.4 6.4 %collective-permute-start.37 = (f32[8,2,1]{0,2,1:T(1,128)S(1)}, f32[8,2,1]{0,2,1:T(1,128)S(1)}, u32[]{:S(2)}, u32[]{:S(2)}) collective-permute-start(f32[8,2,1]{0,2,1:T(1,128)S(1)} %get-tuple-element.153), channel_id=1, source_target_pairs={{32,0},{64,32},{96,64},{128,96},{160,128},{192,160},{224,192},{256... | collective-permute-start | bytes 200 | tf_op jit(solution)/shard_map/ppermute | solution.py:21
  289.9 7.6 %collective-permute-start.36 = (f32[8,2,1]{0,2,1:T(1,128)S(1)}, f32[8,2,1]{0,2,1:T(1,128)S(1)}, u32[]{:S(2)}, u32[]{:S(2)}) collective-permute-start(f32[8,2,1]{0,2,1:T(1,128)S(1)} %get-tuple-element.152), channel_id=1, source_target_pairs={{0,32},{32,64},{64,96},{96,128},{128,160},{160,192},{192,224},{224... | collective-permute-start | bytes 200 | tf_op jit(solution)/shard_map/ppermute | solution.py:20
  326.6 6.5 %collective-permute-start.41 = (f32[8,2,1]{0,2,1:T(1,128)S(1)}, f32[8,2,1]{0,2,1:T(1,128)S(1)}, u32[]{:S(2)}, u32[]{:S(2)}) collective-permute-start(f32[8,2,1]{0,2,1:T(1,128)S(1)} %get-tuple-element.151), channel_id=1, source_target_pairs={{32,0},{64,32},{96,64},{128,96},{160,128},{192,160},{224,192},{256... | collective-permute-start | bytes 200 | tf_op jit(solution)/shard_map/ppermute | solution.py:21
  331.2 7.6 %collective-permute-start.40 = (f32[8,2,1]{0,2,1:T(1,128)S(1)}, f32[8,2,1]{0,2,1:T(1,128)S(1)}, u32[]{:S(2)}, u32[]{:S(2)}) collective-permute-start(f32[8,2,1]{0,2,1:T(1,128)S(1)} %get-tuple-element.150), channel_id=1, source_target_pairs={{0,32},{32,64},{64,96},{96,128},{128,160},{160,192},{192,224},{224... | collective-permute-start | bytes 200 | tf_op jit(solution)/shard_map/ppermute | solution.py:20
  367.3 6.5 %collective-permute-start.45 = (f32[8,2,1]{0,2,1:T(1,128)S(1)}, f32[8,2,1]{0,2,1:T(1,128)S(1)}, u32[]{:S(2)}, u32[]{:S(2)}) collective-permute-start(f32[8,2,1]{0,2,1:T(1,128)S(1)} %get-tuple-element.149), channel_id=1, source_target_pairs={{32,0},{64,32},{96,64},{128,96},{160,128},{192,160},{224,192},{256... | collective-permute-start | bytes 200 | tf_op jit(solution)/shard_map/ppermute | solution.py:21
  371.9 7.6 %collective-permute-start.44 = (f32[8,2,1]{0,2,1:T(1,128)S(1)}, f32[8,2,1]{0,2,1:T(1,128)S(1)}, u32[]{:S(2)}, u32[]{:S(2)}) collective-permute-start(f32[8,2,1]{0,2,1:T(1,128)S(1)} %get-tuple-element.148), channel_id=1, source_target_pairs={{0,32},{32,64},{64,96},{96,128},{128,160},{160,192},{192,224},{224... | collective-permute-start | bytes 200 | tf_op jit(solution)/shard_map/ppermute | solution.py:20
  407.3 6.5 %collective-permute-start.49 = (f32[8,4,1]{0,2,1:T(1,128)S(1)}, f32[8,4,1]{0,2,1:T(1,128)S(1)}, u32[]{:S(2)}, u32[]{:S(2)}) collective-permute-start(f32[8,4,1]{0,2,1:T(1,128)S(1)} %get-tuple-element.119), channel_id=1, source_target_pairs={{32,0},{64,32},{96,64},{128,96},{160,128},{192,160},{224,192},{256... | collective-permute-start | bytes 392 | tf_op jit(solution)/shard_map/ppermute | solution.py:21
  411.9 7.6 %collective-permute-start.48 = (f32[8,4,1]{0,2,1:T(1,128)S(1)}, f32[8,4,1]{0,2,1:T(1,128)S(1)}, u32[]{:S(2)}, u32[]{:S(2)}) collective-permute-start(f32[8,4,1]{0,2,1:T(1,128)S(1)} %get-tuple-element.118), channel_id=1, source_target_pairs={{0,32},{32,64},{64,96},{96,128},{128,160},{160,192},{192,224},{224... | collective-permute-start | bytes 392 | tf_op jit(solution)/shard_map/ppermute | solution.py:20
  449.8 6.4 %collective-permute-start.53 = (f32[8,8,1]{2,1,0:T(8,128)S(1)}, f32[8,8,1]{2,1,0:T(8,128)S(1)}, u32[]{:S(2)}, u32[]{:S(2)}) collective-permute-start(f32[8,8,1]{2,1,0:T(8,128)S(1)} %get-tuple-element.143), channel_id=1, source_target_pairs={{32,0},{64,32},{96,64},{128,96},{160,128},{192,160},{224,192},{256... | collective-permute-start | bytes 776 | tf_op jit(solution)/shard_map/ppermute | solution.py:21
  454.3 7.9 %collective-permute-start.52 = (f32[8,8,1]{2,1,0:T(8,128)S(1)}, f32[8,8,1]{2,1,0:T(8,128)S(1)}, u32[]{:S(2)}, u32[]{:S(2)}) collective-permute-start(f32[8,8,1]{2,1,0:T(8,128)S(1)} %get-tuple-element.142), channel_id=1, source_target_pairs={{0,32},{32,64},{64,96},{96,128},{128,160},{160,192},{192,224},{224... | collective-permute-start | bytes 776 | tf_op jit(solution)/shard_map/ppermute | solution.py:20
  493.7 6.5 %collective-permute-start.57 = (f32[8,16,1]{2,1,0:T(8,128)S(1)}, f32[8,16,1]{2,1,0:T(8,128)S(1)}, u32[]{:S(2)}, u32[]{:S(2)}) collective-permute-start(f32[8,16,1]{2,1,0:T(8,128)S(1)} %get-tuple-element.115), channel_id=1, source_target_pairs={{32,0},{64,32},{96,64},{128,96},{160,128},{192,160},{224,192},{256... | collective-permute-start | bytes 1544 | tf_op jit(solution)/shard_map/ppermute | solution.py:21
  498.3 8.3 %collective-permute-start.56 = (f32[8,16,1]{2,1,0:T(8,128)S(1)}, f32[8,16,1]{2,1,0:T(8,128)S(1)}, u32[]{:S(2)}, u32[]{:S(2)}) collective-permute-start(f32[8,16,1]{2,1,0:T(8,128)S(1)} %get-tuple-element.114), channel_id=1, source_target_pairs={{0,32},{32,64},{64,96},{96,128},{128,160},{160,192},{192,224},{224... | collective-permute-start | bytes 1544 | tf_op jit(solution)/shard_map/ppermute | solution.py:20
  506.7 4.3 collective-permute-start.58
  540.5 6.9 %collective-permute-start.61 = (f32[8,32,1]{2,0,1:T(8,128)S(1)}, f32[8,32,1]{2,0,1:T(8,128)S(1)}, u32[]{:S(2)}, u32[]{:S(2)}) collective-permute-start(f32[8,32,1]{2,0,1:T(8,128)S(1)} %get-tuple-element.77), channel_id=1, source_target_pairs={{32,0},{64,32},{96,64},{128,96},{160,128},{192,160},{224,192},{256... | collective-permute-start | bytes 3080 | tf_op jit(solution)/shard_map/ppermute | solution.py:21
  544.5 9.0 %collective-permute-start.60 = (f32[8,32,1]{2,0,1:T(8,128)S(1)}, f32[8,32,1]{2,0,1:T(8,128)S(1)}, u32[]{:S(2)}, u32[]{:S(2)}) collective-permute-start(f32[8,32,1]{2,0,1:T(8,128)S(1)} %get-tuple-element.76), channel_id=1, source_target_pairs={{0,32},{32,64},{64,96},{96,128},{128,160},{160,192},{192,224},{224... | collective-permute-start | bytes 3080 | tf_op jit(solution)/shard_map/ppermute | solution.py:20
  553.6 4.3 collective-permute-start.62
  582.9 8.1 %collective-permute-start.65 = (f32[8,32,1]{2,0,1:T(8,128)S(1)}, f32[8,32,1]{2,0,1:T(8,128)S(1)}, u32[]{:S(2)}, u32[]{:S(2)}) collective-permute-start(f32[8,32,1]{2,0,1:T(8,128)S(1)} %get-tuple-element.73), channel_id=1, source_target_pairs={{32,0},{64,32},{96,64},{128,96},{160,128},{192,160},{224,192},{256... | collective-permute-start | bytes 3080 | tf_op jit(solution)/shard_map/ppermute | solution.py:21
  588.4 9.0 %collective-permute-start.64 = (f32[8,32,1]{2,0,1:T(8,128)S(1)}, f32[8,32,1]{2,0,1:T(8,128)S(1)}, u32[]{:S(2)}, u32[]{:S(2)}) collective-permute-start(f32[8,32,1]{2,0,1:T(8,128)S(1)} %get-tuple-element.72), channel_id=1, source_target_pairs={{0,32},{32,64},{64,96},{96,128},{128,160},{160,192},{192,224},{224... | collective-permute-start | bytes 3080 | tf_op jit(solution)/shard_map/ppermute | solution.py:20
  597.5 4.3 collective-permute-start.66
  (58 other events, 2310.5 us)
where the time goes:
time: 636 us; the launch traced here: 627 us
  blocking collectives  279 us (44%)
  starting transfers between devices  130 us (20%)
  waiting for transfers between devices  123 us (19%)
  other arithmetic  62.3 us (10%)
  local copies, waits for them, and re-layouts  28.1 us (4%)
    all_gather x12, blocking collectives, local_apply(): gathered = lax.all_gather(rim_rows, 'theta', axis=2, tiled=True)  279 us
    ppermute x34, waiting for transfers between devices, with_halo(): before = lax.ppermute(last, axis, up)  114 us
    ppermute x34, starting transfers between devices, with_halo(): after = lax.ppermute(initial, axis, down)  87.2 us
    ppermute x34, starting transfers between devices, with_halo(): before = lax.ppermute(last, axis, up)  42.4 us
    reduce_sum x8, other arithmetic, coarsen(): values.reshape(shape[0], shape[1] // 2, 2, shape[2] // 2, 2)  14.7 us
  transfers between devices with their start and end apart: 68, of which 42 were waited for; matrix products, arithmetic and copies ran while one was open for 7% of the time, Pallas kernels for 0%

commit v1 on v0

v1 whole, which is shorter than its diff:
```python
import functools

import jax
import jax.numpy as jnp
from jax import lax
from jax.experimental import pallas as pl
from jax.experimental.pallas import tpu as pltpu
from jax.sharding import PartitionSpec as P

MESH = pl.DeviceIdType.MESH
F32 = jnp.float32
NT, NR = 16, 32
HALF = NR // 2
ROWS = 32
GLOBAL_ROWS = NR * ROWS
LANES = 384
LO, GLU, GOD, OWN, GOU, GHD, HI, PHYS = 0, 12, 16, 20, 52, 56, 60, 72
REACH = 3
SEGS = 2 * REACH + 1
SLOTS = 4
NORMAL = {0: 0, 1: 1, 3: -1}
FROM_STATOR = (8, 9, 10, 7)
FROM_ROTOR = (-8, -7, -10, -9)
PER_LEVEL = ("K", "B", "U", "CU", "CL", "CE", "CW", "CZ", "CD", "WD", "E")


def roll(x, shift, axis):
    size = x.shape[axis]
    shift = shift % size
    return x if shift == 0 else pltpu.roll(x, shift, axis)


def tile_row(j, half):
    return (j // 8) * 16 + half * 8 + j % 8


def to_tiles(x):
    nz, rows, columns = x.shape
    x = x.reshape(nz, rows // 8, 8, columns // 128, 128)
    return x.transpose(0, 1, 3, 2, 4).reshape(nz * rows * columns // 128, 128)


def from_tiles(x, shape):
    nz, rows, columns = shape
    x = x.reshape(nz, rows // 8, columns // 128, 8, 128)
    return x.transpose(0, 1, 3, 2, 4).reshape(shape)


def loop_rows(low, high, body, unroll):
    count = (high - low) // unroll

    def step(i, carry):
        for q in range(unroll):
            body(low + i * unroll + q)
        return carry

    if count:
        lax.fori_loop(0, count, step, 0)
    for j in range(low + count * unroll, high):
        body(j)


def kernel(*refs):
    slide_ref, frac_ref, gain_ref, b_ref, k_ref, p_ref, res_ref = refs[:7]
    at = 7
    levels = []
    for _ in range(3):
        levels.append(dict(zip(PER_LEVEL, refs[at : at + len(PER_LEVEL)])))
        at += len(PER_LEVEL)
    (DG, B3S, EP, RT, RC_HI, RC_LO, RG, RGH, WC1, WC2, PK, PB, RN, RX, RB, VP, E3S) = refs[at : at + 17]
    sem_s, sem_r = refs[at + 17 :]

    t = lax.axis_index("theta")
    r = lax.axis_index("rad")
    side = r // HALF
    is_rot = r == HALF - 1
    is_sta = r == HALF
    is_if = is_rot | is_sta
    near = (r >= HALF - REACH) & (r < HALF + REACH)
    slide = slide_ref[0]
    frac = frac_ref[0]
    gain = gain_ref[0]

    def theta(offset):
        return lax.rem(t + offset + 2 * NT, NT)

    lane = lax.broadcasted_iota(jnp.int32, (8, 128), 1)
    lane3 = lax.broadcasted_iota(jnp.int32, (8, LANES), 1)
    axial = lax.broadcasted_iota(jnp.int32, (8, 128), 0)
    K0, B0 = levels[0]["K"], levels[0]["B"]

    zeros3 = jnp.zeros((12, 8, LANES), F32)

    @pl.when(r == 0)
    def _():
        K0[pl.ds(LO, 12)] = zeros3
        B0[pl.ds(LO, 12)] = zeros3

    @pl.when(r == NR - 1)
    def _():
        K0[pl.ds(HI, 12)] = zeros3
        B0[pl.ds(HI, 12)] = zeros3

    RC_LO[...] = jnp.zeros_like(RC_LO)
    RC_HI[...] = jnp.zeros_like(RC_HI)
    RN[...] = jnp.ones_like(RN)
    RX[...] = jnp.ones_like(RX)
    RB[...] = jnp.zeros_like(RB)

    barrier = pltpu.get_barrier_semaphore()
    peers = []
    for dr in range(-REACH, REACH + 1):
        inside = (r + dr >= 0) & (r + dr < NR)
        for dt in (-1, 0, 1):
            if dr or dt:
                peers.append((inside, dt, dr))
        if dr:
            crossing = near & inside & ((r + dr) // HALF != side)
            for o in range(7, 11):
                peers.append((crossing, (1 - 2 * side) * o, dr))
        if dr in (1, 2):
            for o in range(7, 11):
                peers.append((r + dr == HALF - 1, o, dr))
                peers.append((r == HALF, o, dr))
        if dr in (-1, -2):
            for o in range(7, 11):
                peers.append((r == HALF - 1, -o, dr))
                peers.append((r + dr == HALF, -o, dr))
    for o in range(6, 11):
        peers.append((is_if, o, 0))
    for cond, dt, dr in peers:
        peer = (theta(dt), r + dr)

        @pl.when(cond)
        def _(peer=peer):
            pl.semaphore_signal(barrier, inc=1, device_id=peer, device_id_type=MESH)

    for src, dst in ((k_ref, K0), (b_ref, B0)):

        def move(j, src=src, dst=dst):
            for half in range(2):
                dst[OWN + j, :, pl.ds(128 * half, 128)] = src[pl.ds(tile_row(j, half), 8, stride=2 * ROWS), :]

        loop_rows(0, ROWS, move, 8)

    for m in range(4):
        for arr, ref in enumerate((K0, B0)):
            left = right = None
            for q in range(8):
                row = OWN + 8 * m + q
                low = roll(ref[row, :, pl.ds(0, 128)], 16 * q, 1)
                high = roll(ref[row, :, pl.ds(128, 128)], 16 * q + 16, 1)
                here = lane // 16 == q
                left = low if q == 0 else jnp.where(here, low, left)
                right = high if q == 0 else jnp.where(here, high, right)
            EP[0, m, arr] = left
            EP[1, m, arr] = right

    pl.semaphore_wait(barrier, sum(cond.astype(jnp.int32) for cond, _, _ in peers))

    messages = []

    def message(index, send, recv, src, dst, target, start=True):
        copy = pltpu.make_async_remote_copy(
            src_ref=src,
            dst_ref=dst,
            send_sem=sem_s.at[index],
            recv_sem=sem_r.at[index],
            device_id=target,
            device_id_type=MESH,
        )
        if start:
            pl.when(send)(copy.start)
        messages.append((send, copy))
        return lambda: pl.when(recv)(copy.wait_recv)

    always = r >= 0
    down_s, down_r = (r >= 1) & (r != HALF), (r < NR - 1) & (r != HALF - 1)
    up_s, up_r = down_r, down_s
    wide = pl.ds(0, 256)
    w_th = [
        message(0, always, always, EP.at[0], RT.at[0], (theta(-1), r)),
        message(1, always, always, EP.at[1], RT.at[1], (theta(1), r)),
    ]
    w_k = [
        message(2, down_s, down_r, K0.at[pl.ds(OWN, 12), :, wide], K0.at[pl.ds(HI, 12), :, wide], (t, r - 1)),
        message(3, up_s, up_r, K0.at[pl.ds(OWN + 20, 12), :, wide], K0.at[pl.ds(LO, 12), :, wide], (t, r + 1)),
        message(4, down_s, down_r, EP.at[0, pl.ds(0, 2)], RC_HI.at[0], (theta(-1), r - 1)),
        message(5, down_s, down_r, EP.at[1, pl.ds(0, 2)], RC_HI.at[1], (theta(1), r - 1)),
        message(6, up_s, up_r, EP.at[0, pl.ds(2, 2)], RC_LO.at[0], (theta(-1), r + 1)),
        message(7, up_s, up_r, EP.at[1, pl.ds(2, 2)], RC_LO.at[1], (theta(1), r + 1)),
    ]
    w_b = [
        message(8, down_s, down_r, B0.at[pl.ds(OWN, 12), :, wide], B0.at[pl.ds(HI, 12), :, wide], (t, r - 1)),
        message(9, up_s, up_r, B0.at[pl.ds(OWN + 20, 12), :, wide], B0.at[pl.ds(LO, 12), :, wide], (t, r + 1)),
    ]
    w_i = []

    sgn = 1 - 2 * side
    th = {o: theta(o) for o in (-1, 1, 8)}
    th_far = {"g2": theta(-9 * sgn), "ge": theta(-10 + 17 * side), "gw": theta(-7 + 17 * side), "c2": theta(9 * sgn)}

    facing = OWN + 20 * (1 - side)
    facing4 = OWN + 28 * (1 - side)
    group4 = 3 * (1 - side)
    other = NR - 1 - r
    ghost = GOD + (GOU - GOD) * side
    own4 = K0.at[pl.ds(facing4, 4), :, wide]
    items = [
        (own4, K0.at[pl.ds(ghost, 4), :, wide], (t, other)),
        (EP.at[0, group4, 0], RG.at[0], (th[-1], other)),
        (EP.at[1, group4, 0], RG.at[1], (th[1], other)),
        (own4, WC1.at[pl.ds(24, 4)], (th[8], r)),
        (own4, WC2.at[pl.ds(24, 4)], (th_far["g2"], r)),
        (EP.at[0, group4, 0], RGH.at[0], (th_far["ge"], r)),
        (EP.at[1, group4, 0], RGH.at[1], (th_far["gw"], r)),
        (K0.at[pl.ds(facing, 12), :, wide], WC1.at[pl.ds(0, 12)], (th[8], other)),
        (K0.at[pl.ds(facing, 12), :, wide], WC2.at[pl.ds(0, 12)], (th_far["c2"], other)),
        (B0.at[pl.ds(facing, 12), :, wide], WC1.at[pl.ds(12, 12)], (th[8], other)),
        (B0.at[pl.ds(facing, 12), :, wide], WC2.at[pl.ds(12, 12)], (th_far["c2"], other)),
    ]
    for n, (src, dst, target) in enumerate(items):
        w_i.append(message(10 + n, is_if, is_if, src, dst, target))

    cross_corners = []
    for part, (cond, dst, first) in enumerate(((is_sta, RC_HI, 0), (is_rot, RC_LO, 2))):
        other = r - 1 if part == 0 else r + 1
        offs = (-10, -7) if part == 0 else (7, 10)
        got = is_rot if part == 0 else is_sta
        for e in range(2):
            cross_corners.append(
                message(
                    (4 if part == 0 else 6) + e,
                    cond,
                    got,
                    EP.at[e, pl.ds(first, 2)],
                    dst.at[e],
                    (theta(offs[e]), other),
                )
            )

    def pairs(x, cell):
        width = x.shape[-1]
        pick = (lax.broadcasted_iota(jnp.int32, x.shape, x.ndim - 1) // cell) % 2 == 1
        return x + jnp.where(pick, roll(x, cell, x.ndim - 1), roll(x, width - cell, x.ndim - 1))

    gather_index = (lane % 16) * 8

    def pack(rows):
        out = None
        for q, x in enumerate(rows):
            for half in range(2):
                part = jnp.take_along_axis(x[:, 128 * half : 128 * half + 128], gather_index, axis=1)
                out = part if out is None else jnp.where(lane // 16 == 2 * q + half, part, out)
        return out

    own3 = []
    for j in range(4):
        k2 = []
        for i in range(2):
            k1 = []
            for h in range(2):
                row = OWN + 8 * j + 4 * i + 2 * h
                k1.append(0.25 * pairs(K0[row, :, wide] + K0[row + 1, :, wide], 1))
            k2.append(0.25 * pairs(k1[0] + k1[1], 2))
        own3.append(0.25 * pairs(k2[0] + k2[1], 4))
    PK[...] = pack(own3)

    base_n, base_x, base_b = 21, 21 + SEGS * SLOTS, 21 + 2 * SEGS * SLOTS
    w_n, w_x = [], []
    for dr in range(-REACH, REACH + 1):
        inside_s = (r + dr >= 0) & (r + dr < NR)
        inside_r = (r - dr >= 0) & (r - dr < NR)
        seg = REACH - dr
        for slot, off in NORMAL.items():
            if dr or off:
                w_n.append(
                    message(
                        base_n + seg * SLOTS + slot, inside_s, inside_r, PK, RN.at[seg, slot], (theta(-off), r + dr)
                    )
                )
        to, fro = r + dr, r - dr
        to_rot = (to < HALF) & (to >= HALF - REACH) & (r >= HALF - 1)
        to_sta = (to >= HALF) & (to < HALF + REACH) & (r <= HALF)
        got = ((r < HALF) & (r >= HALF - REACH) & (fro >= HALF - 1)) | (
            (r >= HALF) & (r < HALF + REACH) & (fro <= HALF)
        )
        to_side = (r + dr) // HALF
        for slot in range(SLOTS):
            off = -FROM_STATOR[slot] + to_side * (FROM_STATOR[slot] - FROM_ROTOR[slot])
            w_x.append(
                message(
                    base_x + seg * SLOTS + slot, to_rot | to_sta, got, PK, RX.at[seg, slot], (theta(off), r + dr)
                )
            )
    RN[REACH, 0] = PK[...]

    def third(left_pack, right_pack, q):
        return jnp.where(lane < 64, roll(left_pack, -16 * q, 1), roll(right_pack, 112 - 16 * q, 1))

    halo = pl.ds(256, 128)
    for w in w_th:
        w()
    for m in range(4):
        for arr, ref in enumerate((K0, B0)):
            for q in range(8):
                ref[OWN + 8 * m + q, :, halo] = third(RT[0, m, arr], RT[1, m, arr], q)
    for w in w_k:
        w()
    for w in cross_corners:
        w()
    for w in w_b:
        w()
    for j in range(12):
        for arr, ref in enumerate((K0, B0)):
            m, q = divmod(j, 8)
            ref[HI + j, :, halo] = third(RC_HI[0, m, arr], RC_HI[1, m, arr], q)
            m, q = divmod(4 + j, 8)
            ref[LO + j, :, halo] = third(RC_LO[0, m, arr], RC_LO[1, m, arr], q)

    fine = slide - NT * 256 // 2
    d4 = (fine // 4) * 4
    q4 = d4 % 128
    far = d4 >= 128
    back4 = lax.rem(128 - q4, 128)

    for w in w_i:
        w()

    def window(tiles, sign):
        if sign > 0:
            tiles = [jnp.where(far, tiles[(i + 1) % 5], tiles[i]) for i in range(5)]
            turned = [pltpu.roll(x, back4, 1) for x in tiles]
            keep = lane < 128 - q4
            out = [jnp.where(keep, turned[i], turned[(i + 1) % 5]) for i in (0, 1, 2, 4)]
        else:
            tiles = [jnp.where(far, tiles[(i + 4) % 5], tiles[i]) for i in range(5)]
            turned = [pltpu.roll(x, q4, 1) for x in tiles]
            keep = lane >= q4
            out = [jnp.where(keep, turned[i], turned[(i + 4) % 5]) for i in (0, 1, 2, 4)]
        return out[0], out[1], jnp.where(lane < 64, out[2], out[3])

    def fill(sign, dst_k, dst_ghost):
        for j in range(28):
            if j < 24:
                ref, row = ((K0, B0)[j // 12], dst_k + j % 12)
                edge = ref[row, :, halo]
            else:
                ref, row = (K0, dst_ghost + j - 24)
                edge = third(RGH[0], RGH[1], j - 24 + (4 if sign > 0 else 0))
            a = [WC1[j, :, pl.ds(0, 128)], WC1[j, :, pl.ds(128, 128)]]
            b = [WC2[j, :, pl.ds(0, 128)], WC2[j, :, pl.ds(128, 128)]]
            tiles = a + b + [edge] if sign > 0 else a + [edge] + b
            for i, x in enumerate(window(tiles, sign)):
                ref[row, :, pl.ds(128 * i, 128)] = x

    @pl.when(is_rot)
    def _():
        fill(1, HI, GHD)
        for j in range(4):
            K0[GOU + j, :, halo] = third(RG[0], RG[1], j)

    @pl.when(is_sta)
    def _():
        fill(-1, LO, GLU)
        for j in range(4):
            K0[GOD + j, :, halo] = third(RG[0], RG[1], 4 + j)

    @pl.when(jnp.logical_not(is_rot))
    def _():
        K0[pl.ds(GOU, 4)] = K0[pl.ds(HI, 4)]
        K0[pl.ds(GHD, 4)] = K0[pl.ds(OWN + 28, 4)]

    @pl.when(jnp.logical_not(is_sta))
    def _():
        K0[pl.ds(GLU, 4)] = K0[pl.ds(OWN, 4)]
        K0[pl.ds(GOD, 4)] = K0[pl.ds(LO + 8, 4)]

    for level in (1, 2):
        fine_k, coarse_k = levels[level - 1]["K"], levels[level]["K"]

        def down_k(j, fine_k=fine_k, coarse_k=coarse_k, cell=1 << (level - 1)):
            coarse_k[j] = 0.25 * pairs(fine_k[2 * j] + fine_k[2 * j + 1], cell)

        loop_rows(0, PHYS >> level, down_k, 4)

    top = axial < 7
    low_ok, high_ok = r > 0, r < NR - 1

    def coefficients(level, seg, low, high):
        A = levels[level]
        rows_level = GLOBAL_ROWS >> level
        inv = 1.0 / rows_level
        cell = 1 << level
        start = {"lo": LO + 12, "own": OWN, "hi": HI - 32}[seg] >> level
        ok = {"lo": low_ok, "own": None, "hi": high_ok}[seg]

        def body(j):
            pos = r * (ROWS >> level) + j - start
            posf = pos.astype(F32)
            hu = 0.5 * (1.0 + (posf + 1.0) * inv) * jnp.where(pos == rows_level // 2 - 1, gain, 1.0)
            hl = 0.5 * (1.0 + posf * inv) * jnp.where(pos == rows_level // 2, gain, 1.0)
            rc = 1.0 + (posf + 0.5) * inv
            hc1 = 0.5 / jnp.full((8, 128), rc, F32)
            hz1 = jnp.where(top, 0.5 * rc, 0.0)
            hc = jnp.concatenate([hc1] * 3, axis=1)
            hz = jnp.concatenate([hz1] * 3, axis=1)
            k = A["K"][j]
            ce = (k + roll(k, -cell, 1)) * hc
            cw = roll(ce, cell, 1)
            cu = (k + A["K"][j + 1]) * hu
            cl = (k + A["K"][j - 1]) * hl
            cz = (k + roll(k, -1, 0)) * hz
            cd = roll(cz, 1, 0)
            diag = cu + cl + ce + cw + cz + cd
            wd = 0.8 / diag
            if ok is not None:
                wd = jnp.where(ok, wd, 0.0)
            A["CU"][j], A["CL"][j], A["CE"][j], A["CW"][j], A["CZ"][j], A["CD"][j] = cu, cl, ce, cw, cz, cd
            A["WD"][j] = wd
            if level == 0:
                A["U"][j] = wd * A["B"][j]
                if seg == "own":
                    DG[j - OWN] = diag

        loop_rows(low, high, body, 2)

    def spans(level, halo_rows):
        lo, own, hi = LO + 12 >> level, OWN >> level, HI >> level
        out = [("own", own, own + (ROWS >> level))]
        if halo_rows:
            out = [("lo", lo - halo_rows, lo)] + out + [("hi", hi, hi + halo_rows)]
        return out

    for level, halo_rows in ((0, 11), (1, 5), (2, 2)):
        for seg, low, high in spans(level, halo_rows):
            coefficients(level, seg, low, high)

    def weights(active, shift, count):
        out = []
        for i in range(count):
            w = jnp.where(shift == i, 1.0 - frac, 0.0) + jnp.where(shift == i - 1, frac, 0.0)
            out.append(jnp.where(active, w, 1.0 if i == 0 else 0.0))
        return out

    shifts = (fine % 4, (fine // 2) % 2, 0 * fine)
    up_w = [weights(is_rot, shifts[level], (5, 3, 2)[level]) for level in range(3)]
    low_w = [weights(is_sta, shifts[level], (5, 3, 2)[level]) for level in range(3)]

    def mix(x, w, step):
        out = w[0] * x
        for i in range(1, len(w)):
            out = out + w[i] * roll(x, i * step, x.ndim - 1)
        return out

    def ghosts(field, level):
        cell = 1 << level
        lo_end, own, own_end, hi = LO + 12 >> level, OWN >> level, GOU >> level, HI >> level
        field[own_end] = mix(field[hi], up_w[level], -cell)
        field[hi - 1] = mix(field[own_end - 1], up_w[level], cell)
        field[lo_end] = mix(field[own], low_w[level], -cell)
        field[own - 1] = mix(field[lo_end - 1], low_w[level], cell)

    def neighbours(level, field, j):
        A = levels[level]
        cell = 1 << level
        v = field[j]
        return (
            A["CU"][j] * field[j + 1]
            + A["CL"][j] * field[j - 1]
            + A["CE"][j] * roll(v, -cell, 1)
            + A["CW"][j] * roll(v, cell, 1)
            + A["CZ"][j] * roll(v, -1, 0)
            + A["CD"][j] * roll(v, 1, 0)
        )

    for level in range(3):
        A = levels[level]
        if level:

            def first(j, A=A):
                A["U"][j] = A["WD"][j] * A["B"][j]

            for seg, low, high in spans(level, (11, 5, 2)[level]):
                loop_rows(low, high, first, 2)
        ghosts(A["U"], level)

        def restrict(j, A=A, level=level):
            x = 0.2 * (A["B"][2 * j] + A["B"][2 * j + 1])
            x = x + (neighbours(level, A["U"], 2 * j) + neighbours(level, A["U"], 2 * j + 1))
            x = pairs(x, 1 << level)
            if level < 2:
                levels[level + 1]["B"][j] = x
            else:
                B3S[j - (OWN >> 3 if OWN % 8 == 0 else 0)] = x

        if level < 2:
            for seg, low, high in spans(level + 1, (5, 2)[level]):
                loop_rows(low, high, restrict, 1)
        else:
            for j in range(4):
                x = None
                for i in range(2):
                    row = (OWN >> 2) + 2 * j + i
                    y = 0.2 * A["B"][row] + neighbours(2, A["U"], row)
                    x = y if x is None else x + y
                B3S[j] = pairs(x, 4)

    PB[...] = pack([B3S[j, :, wide] for j in range(4)])
    RB[REACH, 0] = PB[...]
    w_p = []
    for dr in range(-REACH, REACH + 1):
        inside_s = (r + dr >= 0) & (r + dr < NR)
        inside_r = (r - dr >= 0) & (r - dr < NR)
        seg = REACH - dr
        same_s = (r + dr) // HALF == side
        same_r = (r - dr) // HALF == side
        to_side = (r + dr) // HALF
        for slot in range(SLOTS):
            index = base_b + seg * SLOTS + slot
            if slot in NORMAL and (dr or slot):
                w_p.append(
                    message(
                        index, inside_s & same_s, inside_r & same_r, PB, RB.at[seg, slot], (theta(-NORMAL[slot]), r + dr)
                    )
                )
            if dr:
                off = -FROM_STATOR[slot] + to_side * (FROM_STATOR[slot] - FROM_ROTOR[slot])
                w_p.append(
                    message(
                        index,
                        inside_s & jnp.logical_not(same_s),
                        inside_r & jnp.logical_not(same_r),
                        PB,
                        RB.at[seg, slot],
                        (theta(off), r + dr),
                    )
                )

    count3 = 4 * SEGS
    d3 = (fine // 16) * 2
    sgn_x = jnp.where(side == 0, lax.rem(128 - d3, 128), d3)

    def unpack(ref):
        tiles = [ref[:, o] for o in range(SLOTS)]
        lane7 = lax.broadcasted_iota(jnp.int32, (SEGS, 8, 128), 2) // 32
        rows = []
        for q in range(4):
            out = roll(tiles[0], -32 * q, 2)
            for o in range(1, SLOTS):
                out = jnp.where(lane7 == o, roll(tiles[o], 32 * (o - q), 2), out)
            rows.append(out)
        return jnp.stack(rows, axis=1).reshape(count3, 8, 128)

    def turn(x):
        return pltpu.roll(x, sgn_x, 2)

    for w in w_n + w_x:
        w()
    kn = unpack(RN)
    kx = turn(unpack(RX))

    far_off = jnp.where(near, side, 1 << 20)

    def coefficients_patch(kn, kx, rows, level, cell):
        rows_level = GLOBAL_ROWS >> level
        inv = 1.0 / rows_level
        pos = (r - REACH) * (ROWS >> level) + lax.broadcasted_iota(jnp.int32, (rows, 8, 128), 0)
        ok = (pos >= 0) & (pos < rows_level)
        beyond = (pos - rows_level // 2) * (1 - 2 * side) >= far_off
        posf = pos.astype(F32)
        hu = 0.5 * (1.0 + (posf + 1.0) * inv) * jnp.where(pos == rows_level // 2 - 1, gain, 1.0)
        hl = 0.5 * (1.0 + posf * inv) * jnp.where(pos == rows_level // 2, gain, 1.0)
        rc = 1.0 + (posf + 0.5) * inv
        hc = 0.5 / rc
        hz = jnp.where(lax.broadcasted_iota(jnp.int32, (rows, 8, 128), 1) < 7, 0.5 * rc, 0.0)
        k = jnp.where(beyond, kx, kn)
        ku = jnp.where(beyond, jnp.concatenate([kx[1:], kx[:1]], 0), jnp.concatenate([kn[1:], kn[:1]], 0))
        kd = jnp.where(beyond, jnp.concatenate([kx[-1:], kx[:-1]], 0), jnp.concatenate([kn[-1:], kn[:-1]], 0))
        ku = jnp.where(pos == rows_level - 1, 0.0, ku)
        kd = jnp.where(pos == 0, 0.0, kd)
        ce = (k + roll(k, -cell, 2)) * hc
        cw = roll(ce, cell, 2)
        cu = (k + ku) * hu
        cl = (k + kd) * hl
        cz = (k + roll(k, -1, 1)) * hz
        cd = roll(cz, 1, 1)
        wd = jnp.where(ok, 0.8 / (cu + cl + ce + cw + cz + cd), 0.0)
        return (cu, cl, ce, cw, cz, cd, wd, beyond)

    def coarse_k(x):
        y = x.reshape(x.shape[0] // 2, 2, 8, 128)
        return 0.25 * pairs(y[:, 0] + y[:, 1], 1)

    C3 = coefficients_patch(kn, kx, count3, 3, 1)
    C4 = coefficients_patch(coarse_k(kn), coarse_k(kx), count3 // 2, 4, 2)

    odd = (fine // 8) % 2
    w3 = weights(r >= 0, odd, 3)
    w4 = weights(r >= 0, 0 * odd, 2)

    def neighbours_patch(C, v, step, w, cell):
        n = v.shape[0]
        edge = lax.rem(HALF - r + REACH + 4 * SEGS, SEGS) * step
        VP[pl.ds(0, n)] = v
        over = mix(VP[edge], w, -cell)
        under = mix(VP[lax.rem(edge + n - 1, n)], w, cell)
        row = lax.broadcasted_iota(jnp.int32, v.shape, 0)
        vu = jnp.concatenate([v[1:], v[:1]], 0)
        vd = jnp.concatenate([v[-1:], v[:-1]], 0)
        mark = jnp.where(near, edge, -8)
        vu = jnp.where(row == mark - 1, over[None], vu)
        vd = jnp.where(row == mark, under[None], vd)
        return (
            C[0] * vu
            + C[1] * vd
            + C[2] * roll(v, -cell, 2)
            + C[3] * roll(v, cell, 2)
            + C[4] * roll(v, -1, 1)
            + C[5] * roll(v, 1, 1)
        )

    for w in w_p:
        w()
    b3 = unpack(RB)
    b3 = jnp.where(C3[7], turn(b3), b3)
    u3 = C3[6] * b3
    x = 0.2 * b3 + neighbours_patch(C3, u3, 4, w3, 1)
    x = x.reshape(count3 // 2, 2, 8, 128)
    b4 = pairs(x[:, 0] + x[:, 1], 1)
    v4 = C4[6] * b4
    for _ in range(3):
        v4 = 0.2 * v4 + C4[6] * (b4 + neighbours_patch(C4, v4, 2, w4, 2))
    up4 = jnp.broadcast_to(v4[:, None], (count3 // 2, 2, 8, 128)).reshape(count3, 8, 128)
    v3 = u3 + up4
    e3 = 0.2 * v3 + C3[6] * (b3 + neighbours_patch(C3, v3, 4, w3, 1))

    delta = (fine // 4) % 4 * 4
    first_row = 4 * REACH - 1
    for j in range(6):
        if j == 0:
            shift = jnp.where(is_sta, -delta, 0)
        elif j == 5:
            shift = jnp.where(is_rot, delta, 0)
        else:
            shift = 0
        for i in range(3):
            signed = lane + 128 * i
            if i == 2:
                signed = jnp.where(lane < 64, signed, signed - LANES)
            index = ((signed + shift + 1024) // 8) % 128
            E3S[j, :, pl.ds(128 * i, 128)] = jnp.take_along_axis(e3[first_row + j], index, axis=1)

    for level in (2, 1, 0):
        A = levels[level]
        low, own, hi = LO + 12 >> level, OWN >> level, HI >> level
        rows = ROWS >> level
        if level == 2:
            A["U"][low - 2] = A["U"][low - 2] + E3S[0]
            A["U"][low - 1] = A["U"][low - 1] + E3S[0]
            for j in range(rows):
                A["U"][own + j] = A["U"][own + j] + E3S[1 + j // 2]
            A["U"][hi] = A["U"][hi] + E3S[5]
            A["U"][hi + 1] = A["U"][hi + 1] + E3S[5]
        else:
            E = levels[level + 1]["E"]

            def add(j, A=A, E=E):
                e = E[j]
                A["U"][2 * j] = A["U"][2 * j] + e
                A["U"][2 * j + 1] = A["U"][2 * j + 1] + e

            add((low >> 1) - 1)
            loop_rows(own >> 1, (own + rows) >> 1, add, 4)
            add(hi >> 1)
        ghosts(A["U"], level)

        def smooth(j, A=A, level=level):
            A["E"][j] = 0.2 * A["U"][j] + A["WD"][j] * (A["B"][j] + neighbours(level, A["U"], j))

        smooth(low - 1)
        loop_rows(own, own + rows, smooth, 2)
        smooth(hi)

    ghosts(levels[0]["E"], 0)

    def finish(j):
        E = levels[0]["E"]
        p = E[OWN + j]
        out = B0[OWN + j] - DG[j] * p + neighbours(0, E, OWN + j)
        for half in range(2):
            place = pl.ds(tile_row(j, half), 8, stride=2 * ROWS)
            p_ref[place, :] = p[:, 128 * half : 128 * half + 128]
            res_ref[place, :] = out[:, 128 * half : 128 * half + 128]

    loop_rows(0, ROWS, finish, 2)

    for send, copy in messages:
        pl.when(send)(copy.wait_send)


def on_device(source, conductance, slide, fraction, gain):
    nz, rows, columns = source.shape
    scratch = []
    for level in range(3):
        scratch += [pltpu.VMEM((PHYS >> level, nz, LANES), F32)] * len(PER_LEVEL)
    tile = (8, 128)
    scratch += [
        pltpu.VMEM((ROWS, nz, LANES), F32),
        pltpu.VMEM((4, nz, LANES), F32),
        pltpu.VMEM((2, 4, 2) + tile, F32),
        pltpu.VMEM((2, 4, 2) + tile, F32),
        pltpu.VMEM((2, 2, 2) + tile, F32),
        pltpu.VMEM((2, 2, 2) + tile, F32),
        pltpu.VMEM((2,) + tile, F32),
        pltpu.VMEM((2,) + tile, F32),
        pltpu.VMEM((28, nz, 256), F32),
        pltpu.VMEM((28, nz, 256), F32),
        pltpu.VMEM(tile, F32),
        pltpu.VMEM(tile, F32),
        pltpu.VMEM((SEGS, SLOTS) + tile, F32),
        pltpu.VMEM((SEGS, SLOTS) + tile, F32),
        pltpu.VMEM((SEGS, SLOTS) + tile, F32),
        pltpu.VMEM((4 * SEGS,) + tile, F32),
        pltpu.VMEM((6, nz, LANES), F32),
    ]
    sems = 21 + 3 * SEGS * SLOTS
    scratch += [pltpu.SemaphoreType.DMA((sems,)), pltpu.SemaphoreType.DMA((sems,))]
    smem = pl.BlockSpec(memory_space=pltpu.SMEM)
    vmem = pl.BlockSpec(memory_space=pltpu.VMEM)
    flat = jax.ShapeDtypeStruct((nz * rows * columns // 128, 128), F32)
    pressure, residual = pl.pallas_call(
        kernel,
        out_shape=(flat, flat),
        in_specs=[smem, smem, smem, vmem, vmem],
        out_specs=(vmem, vmem),
        scratch_shapes=scratch,
        compiler_params=pltpu.CompilerParams(
            collective_id=0, has_side_effects=True, vmem_limit_bytes=48 * 1024 * 1024
        ),
    )(slide, fraction, gain, to_tiles(source), to_tiles(conductance))
    return from_tiles(pressure, source.shape), from_tiles(residual, source.shape)


def solution(mesh):
    spec = P(None, "rad", "theta")
    return jax.shard_map(
        on_device, mesh=mesh, in_specs=(spec, spec, P(), P(), P()), out_specs=(spec, spec), check_vma=False
    )
```

time: 636 us -> 57.3 us (0.09)
  the two profiles are of different devices: /device:TPU:4 before, /device:TPU:193 now
where the time goes in v1:
time: 57.3 us; the launch traced here: 57 us
  Pallas kernels  51.2 us (89%)
  local copies, waits for them, and re-layouts  3.3 us (6%)
  between operations  2.58 us (5%)
    pallas_call x1, Pallas kernels, on_device(): pl.pallas_call(kernel, out_shape=(flat, flat), in_specs=[smem, smem, smem...  51.2 us
    unnamed x6, local copies, waits for them, and re-layouts  3.3 us

profile of v1, /device:TPU:193, one launch (start us, length us, event | category | flops | bytes accessed | tf_op | source)
XLA Modules:
  0.0 57.0 jit_solution(5289178498562724656)
XLA Ops:
  2.6 0.0 copy-start
  2.6 0.9 %copy-done = f32[8,32,256]{2,1,0:T(8,128)S(1)} copy-done((f32[8,32,256]{2,1,0:T(8,128)S(1)}, f32[8,32,256]{2,1,0:T(8,128)}, u32[]{:S(2)}) %copy-start) | copy-done | bytes 262168
  3.5 0.0 copy-start.1
  3.5 0.9 %copy-done.1 = f32[8,32,256]{2,1,0:T(8,128)S(1)} copy-done((f32[8,32,256]{2,1,0:T(8,128)S(1)}, f32[8,32,256]{2,1,0:T(8,128)}, u32[]{:S(2)}) %copy-start.1) | copy-done | bytes 262168
  4.5 51.2 %shard_map.68 = (f32[512,128]{1,0:T(8,128)S(1)}, f32[512,128]{1,0:T(8,128)S(1)}) custom-call(s32[1]{0:T(128)S(6)} %copy.9.refs_0_, f32[1]{0:T(128)S(6)} %copy.10.refs_1_, f32[1]{0:T(128)S(6)} %copy.11.refs_2_, f32[512,128]{1,0:T(8,128)S(1)} %bitcast.20, f32[512,128]{1,0:T(8,128)S(1)} %bitcast.21), custom_call_target="tpu_custom_call" | custom-call | tf_op jit(solution)/shard_map/pallas_call | solution.py:732
  55.6 0.7 %copy.12 = f32[8,32,256]{2,1,0:T(8,128)} copy(f32[8,32,256]{2,1,0:T(8,128)S(1)} %bitcast.23) | data formatting | bytes 524288
  56.3 0.7 %copy.13 = f32[8,32,256]{2,1,0:T(8,128)} copy(f32[8,32,256]{2,1,0:T(8,128)S(1)} %bitcast.22) | data formatting | bytes 524288
Async XLA Ops:
  2.6 1.0 %copy-start = (f32[8,32,256]{2,1,0:T(8,128)S(1)}, f32[8,32,256]{2,1,0:T(8,128)}, u32[]{:S(2)}) copy-start(f32[8,32,256]{2,1,0:T(8,128)} %param.5) | copy-start | bytes 786436
  3.5 0.9 %copy-start.1 = (f32[8,32,256]{2,1,0:T(8,128)S(1)}, f32[8,32,256]{2,1,0:T(8,128)}, u32[]{:S(2)}) copy-start(f32[8,32,256]{2,1,0:T(8,128)} %param.6) | copy-start | bytes 786436

commit v2 on v1

--- a/solution.py
+++ b/solution.py
@@ -20,7 +20,7 @@
 SLOTS = 4
 NORMAL = {0: 0, 1: 1, 3: -1}
 FROM_STATOR = (8, 9, 10, 7)
-FROM_ROTOR = (-8, -7, -10, -9)
+FROM_ROTOR = (-9, -8, -7, -10)
 PER_LEVEL = ("K", "B", "U", "CU", "CL", "CE", "CW", "CZ", "CD", "WD", "E")
 
 
@@ -61,14 +61,18 @@
 
 
 def kernel(*refs):
-    slide_ref, frac_ref, gain_ref, b_ref, k_ref, p_ref, res_ref = refs[:7]
+    slide_ref, frac_ref, gain_ref, b_hbm, k_hbm, p_ref, res_ref = refs[:7]
     at = 7
     levels = []
     for _ in range(3):
         levels.append(dict(zip(PER_LEVEL, refs[at : at + len(PER_LEVEL)])))
         at += len(PER_LEVEL)
     (DG, B3S, EP, RT, RC_HI, RC_LO, RG, RGH, WC1, WC2, PK, PB, RN, RX, RB, VP, E3S) = refs[at : at + 17]
-    sem_s, sem_r = refs[at + 17 :]
+    k_ref, b_ref, sem_s, sem_r, sem_in = refs[at + 17 :]
+
+    loads = [pltpu.make_async_copy(x, y, sem_in.at[i]) for i, (x, y) in enumerate(((k_hbm, k_ref), (b_hbm, b_ref)))]
+    for load in loads:
+        load.start()
 
     t = lax.axis_index("theta")
     r = lax.axis_index("rad")
@@ -108,55 +112,62 @@
     RB[...] = jnp.zeros_like(RB)
 
     barrier = pltpu.get_barrier_semaphore()
-    peers = []
-    for dr in range(-REACH, REACH + 1):
+    sgn = 1 - 2 * side
+    inner = near & jnp.logical_not(is_if)
+    greet, heard = [], []
+
+    def meet(cond, dt, dr):
+        greet.append((cond, dt, dr))
+        heard.append(cond)
+
+    for dr in (1, 2, 3):
+        far_dr = dr * sgn
+        to_inner = is_if & (dr > 1)
+        from_if = inner & ((r + far_dr == HALF - 1) | (r + far_dr == HALF)) & ((r + far_dr) // HALF != side)
+        for o in range(7, 11):
+            if dr > 1:
+                greet.append((to_inner, sgn * o, far_dr))
+            heard.append(from_if)
+    for o in range(7, 11):
+        meet(is_if, sgn * o, sgn)
+        meet((r == HALF - 2) | (r == HALF + 1), sgn * o, 3 * sgn)
+    for o in range(6, 11):
+        meet(is_if, o, 0)
+    for dr in (-3, 3, -2, 2, -1, 1, 0):
         inside = (r + dr >= 0) & (r + dr < NR)
-        for dt in (-1, 0, 1):
+        for dt in (-1, 1, 0) if abs(dr) < 2 else (0,):
             if dr or dt:
-                peers.append((inside, dt, dr))
-        if dr:
-            crossing = near & inside & ((r + dr) // HALF != side)
-            for o in range(7, 11):
-                peers.append((crossing, (1 - 2 * side) * o, dr))
-        if dr in (1, 2):
-            for o in range(7, 11):
-                peers.append((r + dr == HALF - 1, o, dr))
-                peers.append((r == HALF, o, dr))
-        if dr in (-1, -2):
-            for o in range(7, 11):
-                peers.append((r == HALF - 1, -o, dr))
-                peers.append((r + dr == HALF, -o, dr))
-    for o in range(6, 11):
-        peers.append((is_if, o, 0))
-    for cond, dt, dr in peers:
+                meet(inside, dt, dr)
+    for o in (-2, 2):
+        meet(near, o, 0)
+    for cond, dt, dr in greet:
         peer = (theta(dt), r + dr)
 
         @pl.when(cond)
         def _(peer=peer):
             pl.semaphore_signal(barrier, inc=1, device_id=peer, device_id_type=MESH)
 
-    for src, dst in ((k_ref, K0), (b_ref, B0)):
+    for arr, (src, dst) in enumerate(((k_ref, K0), (b_ref, B0))):
+        loads[arr].wait()
 
         def move(j, src=src, dst=dst):
             for half in range(2):
                 dst[OWN + j, :, pl.ds(128 * half, 128)] = src[pl.ds(tile_row(j, half), 8, stride=2 * ROWS), :]
 
-        loop_rows(0, ROWS, move, 8)
-
-    for m in range(4):
-        for arr, ref in enumerate((K0, B0)):
+        loop_rows(0, ROWS, move, ROWS)
+        for m in range(4):
             left = right = None
             for q in range(8):
                 row = OWN + 8 * m + q
-                low = roll(ref[row, :, pl.ds(0, 128)], 16 * q, 1)
-                high = roll(ref[row, :, pl.ds(128, 128)], 16 * q + 16, 1)
+                low = roll(dst[row, :, pl.ds(0, 128)], 16 * q, 1)
+                high = roll(dst[row, :, pl.ds(128, 128)], 16 * q + 16, 1)
                 here = lane // 16 == q
                 left = low if q == 0 else jnp.where(here, low, left)
                 right = high if q == 0 else jnp.where(here, high, right)
             EP[0, m, arr] = left
             EP[1, m, arr] = right
 
-    pl.semaphore_wait(barrier, sum(cond.astype(jnp.int32) for cond, _, _ in peers))
+    pl.semaphore_wait(barrier, sum(cond.astype(jnp.int32) for cond in heard))
 
     messages = []
 
@@ -196,7 +207,6 @@
     ]
     w_i = []
 
-    sgn = 1 - 2 * side
     th = {o: theta(o) for o in (-1, 1, 8)}
     th_far = {"g2": theta(-9 * sgn), "ge": theta(-10 + 17 * side), "gw": theta(-7 + 17 * side), "c2": theta(9 * sgn)}
 
@@ -266,34 +276,36 @@
         own3.append(0.25 * pairs(k2[0] + k2[1], 4))
     PK[...] = pack(own3)
 
-    base_n, base_x, base_b = 21, 21 + SEGS * SLOTS, 21 + 2 * SEGS * SLOTS
-    w_n, w_x = [], []
-    for dr in range(-REACH, REACH + 1):
-        inside_s = (r + dr >= 0) & (r + dr < NR)
-        inside_r = (r - dr >= 0) & (r - dr < NR)
-        seg = REACH - dr
-        for slot, off in NORMAL.items():
-            if dr or off:
-                w_n.append(
-                    message(
-                        base_n + seg * SLOTS + slot, inside_s, inside_r, PK, RN.at[seg, slot], (theta(-off), r + dr)
-                    )
-                )
-        to, fro = r + dr, r - dr
-        to_rot = (to < HALF) & (to >= HALF - REACH) & (r >= HALF - 1)
-        to_sta = (to >= HALF) & (to < HALF + REACH) & (r <= HALF)
-        got = ((r < HALF) & (r >= HALF - REACH) & (fro >= HALF - 1)) | (
-            (r >= HALF) & (r < HALF + REACH) & (fro <= HALF)
-        )
-        to_side = (r + dr) // HALF
-        for slot in range(SLOTS):
-            off = -FROM_STATOR[slot] + to_side * (FROM_STATOR[slot] - FROM_ROTOR[slot])
-            w_x.append(
-                message(
-                    base_x + seg * SLOTS + slot, to_rot | to_sta, got, PK, RX.at[seg, slot], (theta(off), r + dr)
-                )
+    RN[REACH, 0] = PK[...]
+    base_t, base_n, base_x, base_b = 21, 24, 24 + SEGS, 24 + 2 * SEGS
+    w_t = [
+        message(base_t, always, always, PK, RN.at[REACH, 1], (theta(-1), r)),
+        message(base_t + 1, always, always, PK, RN.at[REACH, 3], (theta(1), r)),
+        message(base_t + 2, near, near, PK, RN.at[REACH, 2], (theta(-2), r)),
+    ]
+
+    w_n, w_x = {}, {}
+
+    def send_plain():
+        for dr in (-3, 3, -2, 2, -1, 1):
+            inside_s = (r + dr >= 0) & (r + dr < NR)
+            inside_r = (r - dr >= 0) & (r - dr < NR)
+            seg = REACH - dr
+            w_n[seg] = message(base_n + seg, inside_s, inside_r, RN.at[REACH], RN.at[seg], (t, r + dr))
+
+    def send_across(which):
+        for dr in range(-REACH, REACH + 1):
+            seg = REACH - dr
+            to, fro = r + dr, r - dr
+            to_rot = (to < HALF) & (to >= HALF - REACH) & (r >= HALF - 1)
+            to_sta = (to >= HALF) & (to < HALF + REACH) & (r <= HALF)
+            got = ((r < HALF) & (r >= HALF - REACH) & (fro >= HALF - 1)) | (
+                (r >= HALF) & (r < HALF + REACH) & (fro <= HALF)
             )
-    RN[REACH, 0] = PK[...]
+            off = -FROM_STATOR[0] + ((r + dr) // HALF) * (FROM_STATOR[0] - FROM_ROTOR[0])
+            w_x[seg] = message(
+                base_x + seg, (to_rot | to_sta) & which, got, RN.at[REACH], RX.at[seg], (theta(off), r + dr)
+            )
 
     def third(left_pack, right_pack, q):
         return jnp.where(lane < 64, roll(left_pack, -16 * q, 1), roll(right_pack, 112 - 16 * q, 1))
@@ -305,85 +317,10 @@
         for arr, ref in enumerate((K0, B0)):
             for q in range(8):
                 ref[OWN + 8 * m + q, :, halo] = third(RT[0, m, arr], RT[1, m, arr], q)
-    for w in w_k:
-        w()
-    for w in cross_corners:
-        w()
-    for w in w_b:
-        w()
-    for j in range(12):
-        for arr, ref in enumerate((K0, B0)):
-            m, q = divmod(j, 8)
-            ref[HI + j, :, halo] = third(RC_HI[0, m, arr], RC_HI[1, m, arr], q)
-            m, q = divmod(4 + j, 8)
-            ref[LO + j, :, halo] = third(RC_LO[0, m, arr], RC_LO[1, m, arr], q)
-
-    fine = slide - NT * 256 // 2
-    d4 = (fine // 4) * 4
-    q4 = d4 % 128
-    far = d4 >= 128
-    back4 = lax.rem(128 - q4, 128)
-
-    for w in w_i:
-        w()
-
-    def window(tiles, sign):
-        if sign > 0:
-            tiles = [jnp.where(far, tiles[(i + 1) % 5], tiles[i]) for i in range(5)]
-            turned = [pltpu.roll(x, back4, 1) for x in tiles]
-            keep = lane < 128 - q4
-            out = [jnp.where(keep, turned[i], turned[(i + 1) % 5]) for i in (0, 1, 2, 4)]
-        else:
-            tiles = [jnp.where(far, tiles[(i + 4) % 5], tiles[i]) for i in range(5)]
-            turned = [pltpu.roll(x, q4, 1) for x in tiles]
-            keep = lane >= q4
-            out = [jnp.where(keep, turned[i], turned[(i + 4) % 5]) for i in (0, 1, 2, 4)]
-        return out[0], out[1], jnp.where(lane < 64, out[2], out[3])
-
-    def fill(sign, dst_k, dst_ghost):
-        for j in range(28):
-            if j < 24:
-                ref, row = ((K0, B0)[j // 12], dst_k + j % 12)
-                edge = ref[row, :, halo]
-            else:
-                ref, row = (K0, dst_ghost + j - 24)
-                edge = third(RGH[0], RGH[1], j - 24 + (4 if sign > 0 else 0))
-            a = [WC1[j, :, pl.ds(0, 128)], WC1[j, :, pl.ds(128, 128)]]
-            b = [WC2[j, :, pl.ds(0, 128)], WC2[j, :, pl.ds(128, 128)]]
-            tiles = a + b + [edge] if sign > 0 else a + [edge] + b
-            for i, x in enumerate(window(tiles, sign)):
-                ref[row, :, pl.ds(128 * i, 128)] = x
-
-    @pl.when(is_rot)
-    def _():
-        fill(1, HI, GHD)
-        for j in range(4):
-            K0[GOU + j, :, halo] = third(RG[0], RG[1], j)
-
-    @pl.when(is_sta)
-    def _():
-        fill(-1, LO, GLU)
-        for j in range(4):
-            K0[GOD + j, :, halo] = third(RG[0], RG[1], 4 + j)
-
-    @pl.when(jnp.logical_not(is_rot))
-    def _():
-        K0[pl.ds(GOU, 4)] = K0[pl.ds(HI, 4)]
-        K0[pl.ds(GHD, 4)] = K0[pl.ds(OWN + 28, 4)]
-
-    @pl.when(jnp.logical_not(is_sta))
-    def _():
-        K0[pl.ds(GLU, 4)] = K0[pl.ds(OWN, 4)]
-        K0[pl.ds(GOD, 4)] = K0[pl.ds(LO + 8, 4)]
-
-    for level in (1, 2):
-        fine_k, coarse_k = levels[level - 1]["K"], levels[level]["K"]
-
-        def down_k(j, fine_k=fine_k, coarse_k=coarse_k, cell=1 << (level - 1)):
-            coarse_k[j] = 0.25 * pairs(fine_k[2 * j] + fine_k[2 * j + 1], cell)
-
-        loop_rows(0, PHYS >> level, down_k, 4)
-
+    for w in w_t:
+        w()
+    send_plain()
+    send_across(inner)
     top = axial < 7
     low_ok, high_ok = r > 0, r < NR - 1
 
@@ -423,7 +360,89 @@
                 if seg == "own":
                     DG[j - OWN] = diag
 
-        loop_rows(low, high, body, 2)
+        loop_rows(low, high, body, 8)
+
+    coefficients(0, "own", OWN + 1, OWN + ROWS - 1)
+
+    for w in w_k:
+        w()
+    for w in cross_corners:
+        w()
+    for w in w_b:
+        w()
+    for j in range(12):
+        for arr, ref in enumerate((K0, B0)):
+            m, q = divmod(j, 8)
+            ref[HI + j, :, halo] = third(RC_HI[0, m, arr], RC_HI[1, m, arr], q)
+            m, q = divmod(4 + j, 8)
+            ref[LO + j, :, halo] = third(RC_LO[0, m, arr], RC_LO[1, m, arr], q)
+
+    fine = slide - NT * 256 // 2
+    d4 = (fine // 4) * 4
+    q4 = d4 % 128
+    far = d4 >= 128
+    back4 = lax.rem(128 - q4, 128)
+
+    for w in w_i:
+        w()
+    send_across(is_if)
+
+    def window(tiles, sign):
+        if sign > 0:
+            tiles = [jnp.where(far, tiles[(i + 1) % 5], tiles[i]) for i in range(5)]
+            turned = [pltpu.roll(x, back4, 1) for x in tiles]
+            keep = lane < 128 - q4
+            out = [jnp.where(keep, turned[i], turned[(i + 1) % 5]) for i in (0, 1, 2, 4)]
+        else:
+            tiles = [jnp.where(far, tiles[(i + 4) % 5], tiles[i]) for i in range(5)]
+            turned = [pltpu.roll(x, q4, 1) for x in tiles]
+            keep = lane >= q4
+            out = [jnp.where(keep, turned[i], turned[(i + 4) % 5]) for i in (0, 1, 2, 4)]
+        return out[0], out[1], jnp.where(lane < 64, out[2], out[3])
+
+    def fill(sign, dst_k, dst_ghost):
+        for j in range(28):
+            if j < 24:
+                ref, row = ((K0, B0)[j // 12], dst_k + j % 12)
+                edge = ref[row, :, halo]
+            else:
+                ref, row = (K0, dst_ghost + j - 24)
+                edge = third(RGH[0], RGH[1], j - 24 + (4 if sign > 0 else 0))
+            a = [WC1[j, :, pl.ds(0, 128)], WC1[j, :, pl.ds(128, 128)]]
+            b = [WC2[j, :, pl.ds(0, 128)], WC2[j, :, pl.ds(128, 128)]]
+            tiles = a + b + [edge] if sign > 0 else a + [edge] + b
+            for i, x in enumerate(window(tiles, sign)):
+                ref[row, :, pl.ds(128 * i, 128)] = x
+
+    @pl.when(is_rot)
+    def _():
+        fill(1, HI, GHD)
+        for j in range(4):
+            K0[GOU + j, :, halo] = third(RG[0], RG[1], j)
+
+    @pl.when(is_sta)
+    def _():
+        fill(-1, LO, GLU)
+        for j in range(4):
+            K0[GOD + j, :, halo] = third(RG[0], RG[1], 4 + j)
+
+    @pl.when(jnp.logical_not(is_rot))
+    def _():
+        K0[pl.ds(GOU, 4)] = K0[pl.ds(HI, 4)]
+        K0[pl.ds(GHD, 4)] = K0[pl.ds(OWN + 28, 4)]
+
+    @pl.when(jnp.logical_not(is_sta))
+    def _():
+        K0[pl.ds(GLU, 4)] = K0[pl.ds(OWN, 4)]
+        K0[pl.ds(GOD, 4)] = K0[pl.ds(LO + 8, 4)]
+
+    for level in (1, 2):
+        fine_k, coarse_k = levels[level - 1]["K"], levels[level]["K"]
+
+        def down_k(j, fine_k=fine_k, coarse_k=coarse_k, cell=1 << (level - 1)):
+            coarse_k[j] = 0.25 * pairs(fine_k[2 * j] + fine_k[2 * j + 1], cell)
+
+        loop_rows(0, PHYS >> level, down_k, 4)
 
     def spans(level, halo_rows):
         lo, own, hi = LO + 12 >> level, OWN >> level, HI >> level
@@ -434,7 +453,11 @@
 
     for level, halo_rows in ((0, 11), (1, 5), (2, 2)):
         for seg, low, high in spans(level, halo_rows):
-            coefficients(level, seg, low, high)
+            if level == 0 and seg == "own":
+                coefficients(level, seg, low, low + 1)
+                coefficients(level, seg, high - 1, high)
+            else:
+                coefficients(level, seg, low, high)
 
     def weights(active, shift, count):
         out = []
@@ -482,7 +505,7 @@
                 A["U"][j] = A["WD"][j] * A["B"][j]
 
             for seg, low, high in spans(level, (11, 5, 2)[level]):
-                loop_rows(low, high, first, 2)
+                loop_rows(low, high, first, 8)
         ghosts(A["U"], level)
 
         def restrict(j, A=A, level=level):
@@ -496,7 +519,7 @@
 
         if level < 2:
             for seg, low, high in spans(level + 1, (5, 2)[level]):
-                loop_rows(low, high, restrict, 1)
+                loop_rows(low, high, restrict, 4)
         else:
             for j in range(4):
                 x = None
@@ -506,6 +529,8 @@
                     x = y if x is None else x + y
                 B3S[j] = pairs(x, 4)
 
+    for w in w_n.values():
+        w()
     PB[...] = pack([B3S[j, :, wide] for j in range(4)])
     RB[REACH, 0] = PB[...]
     w_p = []
@@ -539,7 +564,7 @@
 
     count3 = 4 * SEGS
     d3 = (fine // 16) * 2
-    sgn_x = jnp.where(side == 0, lax.rem(128 - d3, 128), d3)
+    sgn_x = jnp.where(side == 0, lax.rem(128 - d3, 128), lax.rem(d3 + 96, 128))
 
     def unpack(ref):
         tiles = [ref[:, o] for o in range(SLOTS)]
@@ -555,7 +580,7 @@
     def turn(x):
         return pltpu.roll(x, sgn_x, 2)
 
-    for w in w_n + w_x:
+    for w in w_x.values():
         w()
     kn = unpack(RN)
     kx = turn(unpack(RX))
@@ -679,7 +704,7 @@
             A["E"][j] = 0.2 * A["U"][j] + A["WD"][j] * (A["B"][j] + neighbours(level, A["U"], j))
 
         smooth(low - 1)
-        loop_rows(own, own + rows, smooth, 2)
+        loop_rows(own, own + rows, smooth, 8)
         smooth(hi)
 
     ghosts(levels[0]["E"], 0)
@@ -693,7 +718,7 @@
             p_ref[place, :] = p[:, 128 * half : 128 * half + 128]
             res_ref[place, :] = out[:, 128 * half : 128 * half + 128]
 
-    loop_rows(0, ROWS, finish, 2)
+    loop_rows(0, ROWS, finish, 8)
 
     for send, copy in messages:
         pl.when(send)(copy.wait_send)
@@ -723,16 +748,19 @@
         pltpu.VMEM((SEGS, SLOTS) + tile, F32),
         pltpu.VMEM((4 * SEGS,) + tile, F32),
         pltpu.VMEM((6, nz, LANES), F32),
+        pltpu.VMEM((nz * rows * columns // 128, 128), F32),
+        pltpu.VMEM((nz * rows * columns // 128, 128), F32),
     ]
-    sems = 21 + 3 * SEGS * SLOTS
-    scratch += [pltpu.SemaphoreType.DMA((sems,)), pltpu.SemaphoreType.DMA((sems,))]
+    sems = 24 + 2 * SEGS + SEGS * SLOTS
+    scratch += [pltpu.SemaphoreType.DMA((n,)) for n in (sems, sems, 2)]
     smem = pl.BlockSpec(memory_space=pltpu.SMEM)
     vmem = pl.BlockSpec(memory_space=pltpu.VMEM)
+    hbm = pl.BlockSpec(memory_space=pl.ANY)
     flat = jax.ShapeDtypeStruct((nz * rows * columns // 128, 128), F32)
     pressure, residual = pl.pallas_call(
         kernel,
         out_shape=(flat, flat),
-        in_specs=[smem, smem, smem, vmem, vmem],
+        in_specs=[smem, smem, smem, hbm, hbm],
         out_specs=(vmem, vmem),
         scratch_shapes=scratch,
         compiler_params=pltpu.CompilerParams(

time: 57.3 us -> 43 us (0.75)
  Pallas kernels: 51.2 us -> 36.9 us
    pallas_call x1, Pallas kernels: 51.2 us -> 36.9 us  [on_device(): pl.pallas_call(kernel, out_shape=(flat, flat), in_specs=[smem, smem, smem...]
where the time goes in v2:
time: 43 us; the launch traced here: 42.8 us
  Pallas kernels  36.9 us (86%)
  local copies, waits for them, and re-layouts  3.3 us (8%)
  between operations  2.58 us (6%)
    pallas_call x1, Pallas kernels, on_device(): pl.pallas_call(kernel, out_shape=(flat, flat), in_specs=[smem, smem, smem...  36.9 us
    unnamed x6, local copies, waits for them, and re-layouts  3.3 us

profile of v2, /device:TPU:193, one launch (start us, length us, event | category | flops | bytes accessed | tf_op | source)
XLA Modules:
  0.0 42.8 jit_solution(4545541974394858332)
XLA Ops:
  2.6 0.0 copy-start
  2.6 0.9 %copy-done = f32[8,32,256]{2,1,0:T(8,128)S(1)} copy-done((f32[8,32,256]{2,1,0:T(8,128)S(1)}, f32[8,32,256]{2,1,0:T(8,128)}, u32[]{:S(2)}) %copy-start) | copy-done | bytes 262168
  3.5 0.0 copy-start.1
  3.5 0.9 %copy-done.1 = f32[8,32,256]{2,1,0:T(8,128)S(1)} copy-done((f32[8,32,256]{2,1,0:T(8,128)S(1)}, f32[8,32,256]{2,1,0:T(8,128)}, u32[]{:S(2)}) %copy-start.1) | copy-done | bytes 262168
  4.5 36.9 %shard_map.68 = (f32[512,128]{1,0:T(8,128)S(1)}, f32[512,128]{1,0:T(8,128)S(1)}) custom-call(s32[1]{0:T(128)S(6)} %copy.9.refs_0_, f32[1]{0:T(128)S(6)} %copy.10.refs_1_, f32[1]{0:T(128)S(6)} %copy.11.refs_2_, f32[512,128]{1,0:T(8,128)S(1)} %bitcast.20, f32[512,128]{1,0:T(8,128)S(1)} %bitcast.21), custom_call_target="tpu_custom_call" | custom-call | tf_op jit(solution)/shard_map/pallas_call | solution.py:760
  41.4 0.7 %copy.12 = f32[8,32,256]{2,1,0:T(8,128)} copy(f32[8,32,256]{2,1,0:T(8,128)S(1)} %bitcast.23) | data formatting | bytes 524288
  42.1 0.7 %copy.13 = f32[8,32,256]{2,1,0:T(8,128)} copy(f32[8,32,256]{2,1,0:T(8,128)S(1)} %bitcast.22) | data formatting | bytes 524288
Async XLA Ops:
  2.6 1.0 %copy-start = (f32[8,32,256]{2,1,0:T(8,128)S(1)}, f32[8,32,256]{2,1,0:T(8,128)}, u32[]{:S(2)}) copy-start(f32[8,32,256]{2,1,0:T(8,128)} %param.5) | copy-start | bytes 786436
  3.5 0.9 %copy-start.1 = (f32[8,32,256]{2,1,0:T(8,128)S(1)}, f32[8,32,256]{2,1,0:T(8,128)}, u32[]{:S(2)}) copy-start(f32[8,32,256]{2,1,0:T(8,128)} %param.6) | copy-start | bytes 786436

commit v3 on v2

--- a/solution.py
+++ b/solution.py
@@ -70,7 +70,8 @@
     (DG, B3S, EP, RT, RC_HI, RC_LO, RG, RGH, WC1, WC2, PK, PB, RN, RX, RB, VP, E3S) = refs[at : at + 17]
     k_ref, b_ref, sem_s, sem_r, sem_in = refs[at + 17 :]
 
-    loads = [pltpu.make_async_copy(x, y, sem_in.at[i]) for i, (x, y) in enumerate(((k_hbm, k_ref), (b_hbm, b_ref)))]
+    moves = ((k_hbm, k_ref), (b_hbm, b_ref))
+    loads = [pltpu.make_async_copy(x, y, sem_in.at[i]) for i, (x, y) in enumerate(moves)]
     for load in loads:
         load.start()
 
@@ -81,9 +82,6 @@
     is_sta = r == HALF
     is_if = is_rot | is_sta
     near = (r >= HALF - REACH) & (r < HALF + REACH)
-    slide = slide_ref[0]
-    frac = frac_ref[0]
-    gain = gain_ref[0]
 
     def theta(offset):
         return lax.rem(t + offset + 2 * NT, NT)
@@ -249,6 +247,10 @@
                 )
             )
 
+    slide = slide_ref[0]
+    frac = frac_ref[0]
+    gain = gain_ref[0]
+
     def pairs(x, cell):
         width = x.shape[-1]
         pick = (lax.broadcasted_iota(jnp.int32, x.shape, x.ndim - 1) // cell) % 2 == 1
@@ -321,6 +323,14 @@
         w()
     send_plain()
     send_across(inner)
+    def down_k(level, low, high):
+        fine_k, coarse_k = levels[level - 1]["K"], levels[level]["K"]
+
+        def body(j):
+            coarse_k[j] = 0.25 * pairs(fine_k[2 * j] + fine_k[2 * j + 1], 1 << (level - 1))
+
+        loop_rows(low, high, body, 8)
+
     top = axial < 7
     low_ok, high_ok = r > 0, r < NR - 1
 
@@ -362,7 +372,88 @@
 
         loop_rows(low, high, body, 8)
 
-    coefficients(0, "own", OWN + 1, OWN + ROWS - 1)
+    fine = slide - NT * 256 // 2
+
+    def weights(active, shift, count):
+        out = []
+        for i in range(count):
+            w = jnp.where(shift == i, 1.0 - frac, 0.0) + jnp.where(shift == i - 1, frac, 0.0)
+            out.append(jnp.where(active, w, 1.0 if i == 0 else 0.0))
+        return out
+
+    shifts = (fine % 4, (fine // 2) % 2, 0 * fine)
+    up_w = [weights(is_rot, shifts[level], (5, 3, 2)[level]) for level in range(3)]
+    low_w = [weights(is_sta, shifts[level], (5, 3, 2)[level]) for level in range(3)]
+
+    def mix(x, w, step):
+        out = w[0] * x
+        for i in range(1, len(w)):
+            out = out + w[i] * roll(x, i * step, x.ndim - 1)
+        return out
+
+    def ghosts(field, level):
+        cell = 1 << level
+        lo_end, own, own_end, hi = LO + 12 >> level, OWN >> level, GOU >> level, HI >> level
+        field[own_end] = mix(field[hi], up_w[level], -cell)
+        field[hi - 1] = mix(field[own_end - 1], up_w[level], cell)
+        field[lo_end] = mix(field[own], low_w[level], -cell)
+        field[own - 1] = mix(field[lo_end - 1], low_w[level], cell)
+
+    def neighbours(level, field, j):
+        A = levels[level]
+        cell = 1 << level
+        v = field[j]
+        return (
+            A["CU"][j] * field[j + 1]
+            + A["CL"][j] * field[j - 1]
+            + A["CE"][j] * roll(v, -cell, 1)
+            + A["CW"][j] * roll(v, cell, 1)
+            + A["CZ"][j] * roll(v, -1, 0)
+            + A["CD"][j] * roll(v, 1, 0)
+        )
+
+    def first(level, low, high):
+        A = levels[level]
+
+        def body(j):
+            A["U"][j] = A["WD"][j] * A["B"][j]
+
+        loop_rows(low, high, body, 8)
+
+    def restrict(level, low, high):
+        A = levels[level]
+
+        def body(j):
+            x = 0.2 * (A["B"][2 * j] + A["B"][2 * j + 1])
+            x = x + (neighbours(level, A["U"], 2 * j) + neighbours(level, A["U"], 2 * j + 1))
+            levels[level + 1]["B"][j] = pairs(x, 1 << level)
+
+        loop_rows(low, high, body, 4)
+
+    def restrict3(rows):
+        A = levels[2]
+        for j in rows:
+            x = None
+            for i in range(2):
+                row = (OWN >> 2) + 2 * j + i
+                y = 0.2 * A["B"][row] + neighbours(2, A["U"], row)
+                x = y if x is None else x + y
+            B3S[j] = pairs(x, 4)
+
+    own0, own1, own2 = OWN, OWN >> 1, OWN >> 2
+    lo0, lo1, lo2 = LO + 12, LO + 12 >> 1, LO + 12 >> 2
+    hi0, hi1, hi2 = HI, HI >> 1, HI >> 2
+
+    down_k(1, own1, own1 + 16)
+    down_k(2, own2, own2 + 8)
+    coefficients(0, "own", own0 + 1, own0 + 31)
+    coefficients(1, "own", own1 + 1, own1 + 15)
+    coefficients(2, "own", own2 + 1, own2 + 7)
+    restrict(0, own1 + 1, own1 + 15)
+    first(1, own1 + 1, own1 + 15)
+    restrict(1, own2 + 1, own2 + 7)
+    first(2, own2 + 1, own2 + 7)
+    restrict3((1, 2))
 
     for w in w_k:
         w()
@@ -377,7 +468,6 @@
             m, q = divmod(4 + j, 8)
             ref[LO + j, :, halo] = third(RC_LO[0, m, arr], RC_LO[1, m, arr], q)
 
-    fine = slide - NT * 256 // 2
     d4 = (fine // 4) * 4
     q4 = d4 % 128
     far = d4 >= 128
@@ -436,105 +526,40 @@
         K0[pl.ds(GLU, 4)] = K0[pl.ds(OWN, 4)]
         K0[pl.ds(GOD, 4)] = K0[pl.ds(LO + 8, 4)]
 
-    for level in (1, 2):
-        fine_k, coarse_k = levels[level - 1]["K"], levels[level]["K"]
-
-        def down_k(j, fine_k=fine_k, coarse_k=coarse_k, cell=1 << (level - 1)):
-            coarse_k[j] = 0.25 * pairs(fine_k[2 * j] + fine_k[2 * j + 1], cell)
-
-        loop_rows(0, PHYS >> level, down_k, 4)
-
-    def spans(level, halo_rows):
-        lo, own, hi = LO + 12 >> level, OWN >> level, HI >> level
-        out = [("own", own, own + (ROWS >> level))]
-        if halo_rows:
-            out = [("lo", lo - halo_rows, lo)] + out + [("hi", hi, hi + halo_rows)]
-        return out
-
-    for level, halo_rows in ((0, 11), (1, 5), (2, 2)):
-        for seg, low, high in spans(level, halo_rows):
-            if level == 0 and seg == "own":
-                coefficients(level, seg, low, low + 1)
-                coefficients(level, seg, high - 1, high)
-            else:
-                coefficients(level, seg, low, high)
-
-    def weights(active, shift, count):
-        out = []
-        for i in range(count):
-            w = jnp.where(shift == i, 1.0 - frac, 0.0) + jnp.where(shift == i - 1, frac, 0.0)
-            out.append(jnp.where(active, w, 1.0 if i == 0 else 0.0))
-        return out
-
-    shifts = (fine % 4, (fine // 2) % 2, 0 * fine)
-    up_w = [weights(is_rot, shifts[level], (5, 3, 2)[level]) for level in range(3)]
-    low_w = [weights(is_sta, shifts[level], (5, 3, 2)[level]) for level in range(3)]
-
-    def mix(x, w, step):
-        out = w[0] * x
-        for i in range(1, len(w)):
-            out = out + w[i] * roll(x, i * step, x.ndim - 1)
-        return out
-
-    def ghosts(field, level):
-        cell = 1 << level
-        lo_end, own, own_end, hi = LO + 12 >> level, OWN >> level, GOU >> level, HI >> level
-        field[own_end] = mix(field[hi], up_w[level], -cell)
-        field[hi - 1] = mix(field[own_end - 1], up_w[level], cell)
-        field[lo_end] = mix(field[own], low_w[level], -cell)
-        field[own - 1] = mix(field[lo_end - 1], low_w[level], cell)
-
-    def neighbours(level, field, j):
-        A = levels[level]
-        cell = 1 << level
-        v = field[j]
-        return (
-            A["CU"][j] * field[j + 1]
-            + A["CL"][j] * field[j - 1]
-            + A["CE"][j] * roll(v, -cell, 1)
-            + A["CW"][j] * roll(v, cell, 1)
-            + A["CZ"][j] * roll(v, -1, 0)
-            + A["CD"][j] * roll(v, 1, 0)
-        )
-
-    for level in range(3):
-        A = levels[level]
-        if level:
-
-            def first(j, A=A):
-                A["U"][j] = A["WD"][j] * A["B"][j]
-
-            for seg, low, high in spans(level, (11, 5, 2)[level]):
-                loop_rows(low, high, first, 8)
-        ghosts(A["U"], level)
-
-        def restrict(j, A=A, level=level):
-            x = 0.2 * (A["B"][2 * j] + A["B"][2 * j + 1])
-            x = x + (neighbours(level, A["U"], 2 * j) + neighbours(level, A["U"], 2 * j + 1))
-            x = pairs(x, 1 << level)
-            if level < 2:
-                levels[level + 1]["B"][j] = x
-            else:
-                B3S[j - (OWN >> 3 if OWN % 8 == 0 else 0)] = x
-
-        if level < 2:
-            for seg, low, high in spans(level + 1, (5, 2)[level]):
-                loop_rows(low, high, restrict, 4)
-        else:
-            for j in range(4):
-                x = None
-                for i in range(2):
-                    row = (OWN >> 2) + 2 * j + i
-                    y = 0.2 * A["B"][row] + neighbours(2, A["U"], row)
-                    x = y if x is None else x + y
-                B3S[j] = pairs(x, 4)
+    for level, low, high, end in ((1, own1, own1 + 16, PHYS >> 1), (2, own2, own2 + 8, PHYS >> 2)):
+        down_k(level, 0, low)
+        down_k(level, high, end)
+    coefficients(0, "own", own0, own0 + 1)
+    coefficients(0, "own", own0 + 31, own0 + 32)
+    coefficients(0, "lo", lo0 - 11, lo0)
+    coefficients(0, "hi", hi0, hi0 + 11)
+    coefficients(1, "own", own1, own1 + 1)
+    coefficients(1, "own", own1 + 15, own1 + 16)
+    coefficients(1, "lo", lo1 - 5, lo1)
+    coefficients(1, "hi", hi1, hi1 + 5)
+    coefficients(2, "own", own2, own2 + 1)
+    coefficients(2, "own", own2 + 7, own2 + 8)
+    coefficients(2, "lo", lo2 - 2, lo2)
+    coefficients(2, "hi", hi2, hi2 + 2)
+    ghosts(levels[0]["U"], 0)
+    for low, high in ((lo1 - 5, lo1), (own1, own1 + 1), (own1 + 15, own1 + 16), (hi1, hi1 + 5)):
+        restrict(0, low, high)
+    for low, high in ((lo1 - 5, lo1), (own1, own1 + 1), (own1 + 15, own1 + 16), (hi1, hi1 + 5)):
+        first(1, low, high)
+    ghosts(levels[1]["U"], 1)
+    for low, high in ((lo2 - 2, lo2), (own2, own2 + 1), (own2 + 7, own2 + 8), (hi2, hi2 + 2)):
+        restrict(1, low, high)
+    for low, high in ((lo2 - 2, lo2), (own2, own2 + 1), (own2 + 7, own2 + 8), (hi2, hi2 + 2)):
+        first(2, low, high)
+    ghosts(levels[2]["U"], 2)
+    restrict3((0, 3))
 
     for w in w_n.values():
         w()
     PB[...] = pack([B3S[j, :, wide] for j in range(4)])
     RB[REACH, 0] = PB[...]
     w_p = []
-    for dr in range(-REACH, REACH + 1):
+    for dr in (-3, 3, -2, 2, -1, 1, 0):
         inside_s = (r + dr >= 0) & (r + dr < NR)
         inside_r = (r - dr >= 0) & (r - dr < NR)
         seg = REACH - dr
@@ -753,20 +778,22 @@
     ]
     sems = 24 + 2 * SEGS + SEGS * SLOTS
     scratch += [pltpu.SemaphoreType.DMA((n,)) for n in (sems, sems, 2)]
+    vmem = pl.BlockSpec(memory_space=pltpu.VMEM)
     smem = pl.BlockSpec(memory_space=pltpu.SMEM)
-    vmem = pl.BlockSpec(memory_space=pltpu.VMEM)
-    hbm = pl.BlockSpec(memory_space=pl.ANY)
+    hbm = pl.BlockSpec(memory_space=pltpu.HBM)
     flat = jax.ShapeDtypeStruct((nz * rows * columns // 128, 128), F32)
+    large = [pltpu.with_memory_space_constraint(to_tiles(x), pltpu.HBM) for x in (source, conductance)]
+    operands = (slide, fraction, gain, *large)
     pressure, residual = pl.pallas_call(
         kernel,
         out_shape=(flat, flat),
-        in_specs=[smem, smem, smem, hbm, hbm],
+        in_specs=[smem] * 3 + [hbm] * 2,
         out_specs=(vmem, vmem),
         scratch_shapes=scratch,
         compiler_params=pltpu.CompilerParams(
             collective_id=0, has_side_effects=True, vmem_limit_bytes=48 * 1024 * 1024
         ),
-    )(slide, fraction, gain, to_tiles(source), to_tiles(conductance))
+    )(*operands)
     return from_tiles(pressure, source.shape), from_tiles(residual, source.shape)
 
 

time: 43 us -> 40.6 us (0.944)
  local copies, waits for them, and re-layouts: 3.3 us -> 1.41 us
  Pallas kernels: 36.9 us -> 36.4 us
    unnamed x6 -> x2, local copies, waits for them, and re-layouts: 3.3 us -> 1.41 us
    pallas_call x1, Pallas kernels: 36.9 us -> 36.4 us  [on_device(): pl.pallas_call(kernel, out_shape=(flat, flat), in_specs=[smem] * 3 + [hbm...]
where the time goes in v3:
time: 40.6 us; the launch traced here: 40.4 us
  Pallas kernels  36.4 us (90%)
  between operations  2.58 us (6%)
  local copies, waits for them, and re-layouts  1.41 us (3%)
    pallas_call x1, Pallas kernels, on_device(): pl.pallas_call(kernel, out_shape=(flat, flat), in_specs=[smem] * 3 + [hbm...  36.4 us
    unnamed x2, local copies, waits for them, and re-layouts  1.41 us

profile of v3, /device:TPU:193, one launch (start us, length us, event | category | flops | bytes accessed | tf_op | source)
XLA Modules:
  0.0 40.4 jit_solution(17224909084931467634)
XLA Ops:
  2.6 36.4 %shard_map.68 = (f32[512,128]{1,0:T(8,128)S(1)}, f32[512,128]{1,0:T(8,128)S(1)}) custom-call(s32[1]{0:T(128)S(6)} %copy.9.refs_0_, f32[1]{0:T(128)S(6)} %copy.10.refs_1_, f32[1]{0:T(128)S(6)} %copy.11.refs_2_, f32[512,128]{1,0:T(8,128)} %bitcast.22, f32[512,128]{1,0:T(8,128)} %bitcast.23), custom_call_target="tpu_custom_call" | custom-call | tf_op jit(solution)/shard_map/pallas_call | solution.py:787
  39.0 0.7 %copy.12 = f32[8,32,256]{2,1,0:T(8,128)} copy(f32[8,32,256]{2,1,0:T(8,128)S(1)} %bitcast.21) | data formatting | bytes 524288
  39.7 0.7 %copy.13 = f32[8,32,256]{2,1,0:T(8,128)} copy(f32[8,32,256]{2,1,0:T(8,128)S(1)} %bitcast.20) | data formatting | bytes 524288

commit v4 on v3

--- a/solution.py
+++ b/solution.py
@@ -334,7 +334,7 @@
     top = axial < 7
     low_ok, high_ok = r > 0, r < NR - 1
 
-    def coefficients(level, seg, low, high):
+    def coefficients(level, seg, low, high, unroll=8):
         A = levels[level]
         rows_level = GLOBAL_ROWS >> level
         inv = 1.0 / rows_level
@@ -370,7 +370,7 @@
                 if seg == "own":
                     DG[j - OWN] = diag
 
-        loop_rows(low, high, body, 8)
+        loop_rows(low, high, body, unroll)
 
     fine = slide - NT * 256 // 2
 
@@ -554,8 +554,6 @@
     ghosts(levels[2]["U"], 2)
     restrict3((0, 3))
 
-    for w in w_n.values():
-        w()
     PB[...] = pack([B3S[j, :, wide] for j in range(4)])
     RB[REACH, 0] = PB[...]
     w_p = []
@@ -605,7 +603,7 @@
     def turn(x):
         return pltpu.roll(x, sgn_x, 2)
 
-    for w in w_x.values():
+    for w in list(w_x.values()) + list(w_n.values()):
         w()
     kn = unpack(RN)
     kx = turn(unpack(RX))

time: 40.6 us -> 37.6 us (0.926)
  Pallas kernels: 36.4 us -> 33.4 us
    pallas_call x1, Pallas kernels: 36.4 us -> 33.4 us  [on_device(): pl.pallas_call(kernel, out_shape=(flat, flat), in_specs=[smem] * 3 + [hbm...]
where the time goes in v4:
time: 37.6 us; the launch traced here: 37.4 us
  Pallas kernels  33.4 us (89%)
  between operations  2.58 us (7%)
  local copies, waits for them, and re-layouts  1.41 us (4%)
    pallas_call x1, Pallas kernels, on_device(): pl.pallas_call(kernel, out_shape=(flat, flat), in_specs=[smem] * 3 + [hbm...  33.4 us
    unnamed x2, local copies, waits for them, and re-layouts  1.41 us

profile of v4, /device:TPU:193, one launch (start us, length us, event | category | flops | bytes accessed | tf_op | source)
XLA Modules:
  0.0 37.4 jit_solution(16865084066079493632)
XLA Ops:
  2.6 33.4 %shard_map.68 = (f32[512,128]{1,0:T(8,128)S(1)}, f32[512,128]{1,0:T(8,128)S(1)}) custom-call(s32[1]{0:T(128)S(6)} %copy.9.refs_0_, f32[1]{0:T(128)S(6)} %copy.10.refs_1_, f32[1]{0:T(128)S(6)} %copy.11.refs_2_, f32[512,128]{1,0:T(8,128)} %bitcast.22, f32[512,128]{1,0:T(8,128)} %bitcast.23), custom_call_target="tpu_custom_call" | custom-call | tf_op jit(solution)/shard_map/pallas_call | solution.py:785
  36.0 0.7 %copy.12 = f32[8,32,256]{2,1,0:T(8,128)} copy(f32[8,32,256]{2,1,0:T(8,128)S(1)} %bitcast.21) | data formatting | bytes 524288
  36.7 0.7 %copy.13 = f32[8,32,256]{2,1,0:T(8,128)} copy(f32[8,32,256]{2,1,0:T(8,128)S(1)} %bitcast.20) | data formatting | bytes 524288

commit v5 on v4

--- a/solution.py
+++ b/solution.py
@@ -556,7 +556,7 @@
 
     PB[...] = pack([B3S[j, :, wide] for j in range(4)])
     RB[REACH, 0] = PB[...]
-    w_p = []
+    w_p, sent = [], []
     for dr in (-3, 3, -2, 2, -1, 1, 0):
         inside_s = (r + dr >= 0) & (r + dr < NR)
         inside_r = (r - dr >= 0) & (r - dr < NR)
@@ -564,26 +564,39 @@
         same_s = (r + dr) // HALF == side
         same_r = (r - dr) // HALF == side
         to_side = (r + dr) // HALF
-        for slot in range(SLOTS):
-            index = base_b + seg * SLOTS + slot
-            if slot in NORMAL and (dr or slot):
-                w_p.append(
-                    message(
-                        index, inside_s & same_s, inside_r & same_r, PB, RB.at[seg, slot], (theta(-NORMAL[slot]), r + dr)
-                    )
+        near_ways = [(slot, off) for slot, off in NORMAL.items() if dr or off]
+        ways = [(inside_s & same_s, inside_r & same_r, [(slot, theta(-off)) for slot, off in near_ways])]
+        if dr:
+            across = [
+                (slot, theta(-FROM_STATOR[slot] + to_side * (FROM_STATOR[slot] - FROM_ROTOR[slot])))
+                for slot in range(SLOTS)
+            ]
+            ways.append((inside_s & jnp.logical_not(same_s), inside_r & jnp.logical_not(same_r), across))
+        for send, recv, targets in ways:
+
+            def copy_of(src, dst, target, seg=seg, dr=dr):
+                return pltpu.make_async_remote_copy(
+                    src_ref=src,
+                    dst_ref=dst,
+                    send_sem=sem_s.at[base_b + seg],
+                    recv_sem=sem_r.at[base_b + seg],
+                    device_id=(target, r + dr),
+                    device_id_type=MESH,
                 )
-            if dr:
-                off = -FROM_STATOR[slot] + to_side * (FROM_STATOR[slot] - FROM_ROTOR[slot])
-                w_p.append(
-                    message(
-                        index,
-                        inside_s & jnp.logical_not(same_s),
-                        inside_r & jnp.logical_not(same_r),
-                        PB,
-                        RB.at[seg, slot],
-                        (theta(off), r + dr),
-                    )
-                )
+
+            copies = [copy_of(PB, RB.at[seg, slot], target) for slot, target in targets]
+
+            @pl.when(send)
+            def _(copies=copies):
+                for copy in copies:
+                    copy.start()
+
+            whole = RB.at[seg, pl.ds(0, len(targets))]
+            both = copy_of(whole, whole, targets[0][1])
+            w_p.append((recv, both))
+            sent.append((send, both))
+    for send, copy in messages:
+        pl.when(send)(copy.wait_send)
 
     count3 = 4 * SEGS
     d3 = (fine // 16) * 2
@@ -668,8 +681,8 @@
             + C[5] * roll(v, 1, 1)
         )
 
-    for w in w_p:
-        w()
+    for recv, both in w_p:
+        pl.when(recv)(both.wait_recv)
     b3 = unpack(RB)
     b3 = jnp.where(C3[7], turn(b3), b3)
     u3 = C3[6] * b3
@@ -735,7 +748,20 @@
     def finish(j):
         E = levels[0]["E"]
         p = E[OWN + j]
-        out = B0[OWN + j] - DG[j] * p + neighbours(0, E, OWN + j)
+        A = levels[0]
+        o = OWN + j
+        east, west = roll(p, -1, 1)[:, :256], roll(p, 1, 1)[:, :256]
+        v = p[:, :256]
+        out = (
+            B0[o, :, wide]
+            - DG[j, :, wide] * v
+            + A["CU"][o, :, wide] * E[o + 1, :, wide]
+            + A["CL"][o, :, wide] * E[o - 1, :, wide]
+            + A["CE"][o, :, wide] * east
+            + A["CW"][o, :, wide] * west
+            + A["CZ"][o, :, wide] * roll(v, -1, 0)
+            + A["CD"][o, :, wide] * roll(v, 1, 0)
+        )
         for half in range(2):
             place = pl.ds(tile_row(j, half), 8, stride=2 * ROWS)
             p_ref[place, :] = p[:, 128 * half : 128 * half + 128]
@@ -743,8 +769,8 @@
 
     loop_rows(0, ROWS, finish, 8)
 
-    for send, copy in messages:
-        pl.when(send)(copy.wait_send)
+    for send, both in sent:
+        pl.when(send)(both.wait_send)
 
 
 def on_device(source, conductance, slide, fraction, gain):
@@ -774,7 +800,7 @@
         pltpu.VMEM((nz * rows * columns // 128, 128), F32),
         pltpu.VMEM((nz * rows * columns // 128, 128), F32),
     ]
-    sems = 24 + 2 * SEGS + SEGS * SLOTS
+    sems = 24 + 3 * SEGS
     scratch += [pltpu.SemaphoreType.DMA((n,)) for n in (sems, sems, 2)]
     vmem = pl.BlockSpec(memory_space=pltpu.VMEM)
     smem = pl.BlockSpec(memory_space=pltpu.SMEM)

time: 37.6 us -> 37.1 us (0.987)
  Pallas kernels: 33.4 us -> 32.9 us
    pallas_call x1, Pallas kernels: 33.4 us -> 32.9 us  [on_device(): pl.pallas_call(kernel, out_shape=(flat, flat), in_specs=[smem] * 3 + [hbm...]
where the time goes in v5:
time: 37.1 us; the launch traced here: 36.9 us
  Pallas kernels  32.9 us (89%)
  between operations  2.58 us (7%)
  local copies, waits for them, and re-layouts  1.41 us (4%)
    pallas_call x1, Pallas kernels, on_device(): pl.pallas_call(kernel, out_shape=(flat, flat), in_specs=[smem] * 3 + [hbm...  32.9 us
    unnamed x2, local copies, waits for them, and re-layouts  1.41 us

profile of v5, /device:TPU:193, one launch (start us, length us, event | category | flops | bytes accessed | tf_op | source)
XLA Modules:
  0.0 36.9 jit_solution(6265850581992408547)
XLA Ops:
  2.6 32.9 %shard_map.68 = (f32[512,128]{1,0:T(8,128)S(1)}, f32[512,128]{1,0:T(8,128)S(1)}) custom-call(s32[1]{0:T(128)S(6)} %copy.9.refs_0_, f32[1]{0:T(128)S(6)} %copy.10.refs_1_, f32[1]{0:T(128)S(6)} %copy.11.refs_2_, f32[512,128]{1,0:T(8,128)} %bitcast.22, f32[512,128]{1,0:T(8,128)} %bitcast.23), custom_call_target="tpu_custom_call" | custom-call | tf_op jit(solution)/shard_map/pallas_call | solution.py:811
  35.5 0.7 %copy.12 = f32[8,32,256]{2,1,0:T(8,128)} copy(f32[8,32,256]{2,1,0:T(8,128)S(1)} %bitcast.21) | data formatting | bytes 524288
  36.2 0.7 %copy.13 = f32[8,32,256]{2,1,0:T(8,128)} copy(f32[8,32,256]{2,1,0:T(8,128)S(1)} %bitcast.20) | data formatting | bytes 524288

commit v6 on v5

--- a/solution.py
+++ b/solution.py
@@ -428,7 +428,7 @@
             x = x + (neighbours(level, A["U"], 2 * j) + neighbours(level, A["U"], 2 * j + 1))
             levels[level + 1]["B"][j] = pairs(x, 1 << level)
 
-        loop_rows(low, high, body, 4)
+        loop_rows(low, high, body, 7)
 
     def restrict3(rows):
         A = levels[2]
@@ -740,7 +740,7 @@
             A["E"][j] = 0.2 * A["U"][j] + A["WD"][j] * (A["B"][j] + neighbours(level, A["U"], j))
 
         smooth(low - 1)
-        loop_rows(own, own + rows, smooth, 8)
+        loop_rows(own, own + rows, smooth, 16)
         smooth(hi)
 
     ghosts(levels[0]["E"], 0)
@@ -767,7 +767,7 @@
             p_ref[place, :] = p[:, 128 * half : 128 * half + 128]
             res_ref[place, :] = out[:, 128 * half : 128 * half + 128]
 
-    loop_rows(0, ROWS, finish, 8)
+    loop_rows(0, ROWS, finish, 32)
 
     for send, both in sent:
         pl.when(send)(both.wait_send)

time: 37.1 us -> 36.4 us (0.981)
  Pallas kernels: 32.9 us -> 32.3 us
    pallas_call x1, Pallas kernels: 32.9 us -> 32.3 us  [on_device(): pl.pallas_call(kernel, out_shape=(flat, flat), in_specs=[smem] * 3 + [hbm...]
where the time goes in v6:
time: 36.4 us; the launch traced here: 36.3 us
  Pallas kernels  32.3 us (89%)
  between operations  2.58 us (7%)
  local copies, waits for them, and re-layouts  1.41 us (4%)
    pallas_call x1, Pallas kernels, on_device(): pl.pallas_call(kernel, out_shape=(flat, flat), in_specs=[smem] * 3 + [hbm...  32.3 us
    unnamed x2, local copies, waits for them, and re-layouts  1.41 us

profile of v6, /device:TPU:193, one launch (start us, length us, event | category | flops | bytes accessed | tf_op | source)
XLA Modules:
  0.0 36.3 jit_solution(1801508987096850226)
XLA Ops:
  2.6 32.3 %shard_map.68 = (f32[512,128]{1,0:T(8,128)S(1)}, f32[512,128]{1,0:T(8,128)S(1)}) custom-call(s32[1]{0:T(128)S(6)} %copy.9.refs_0_, f32[1]{0:T(128)S(6)} %copy.10.refs_1_, f32[1]{0:T(128)S(6)} %copy.11.refs_2_, f32[512,128]{1,0:T(8,128)} %bitcast.22, f32[512,128]{1,0:T(8,128)} %bitcast.23), custom_call_target="tpu_custom_call" | custom-call | tf_op jit(solution)/shard_map/pallas_call | solution.py:811
  34.9 0.7 %copy.12 = f32[8,32,256]{2,1,0:T(8,128)} copy(f32[8,32,256]{2,1,0:T(8,128)S(1)} %bitcast.21) | data formatting | bytes 524288
  35.6 0.7 %copy.13 = f32[8,32,256]{2,1,0:T(8,128)} copy(f32[8,32,256]{2,1,0:T(8,128)S(1)} %bitcast.20) | data formatting | bytes 524288
